TPU v7x, 32 devices: a whole 2x2x4 slice. The times are simulated.
32 devices in a mesh: dp: 8 (over z, x), tensor: 4 (over y, core).
Axes of the slice: x: 2, y: 2, z: 4, core: 2. Of those that a mesh axis runs over, the one named last changes fastest.
Arguments:
- tokens: bfloat16 [7680, 1024], P('dp'), may hold values from -6 to 6
- lengths: int32 [512], P('dp'), may hold values from 2 to 15
- query_weight: bfloat16 [1024, 1024], P(None, 'tensor'), may hold values from -0.1875 to 0.1875
- key_weight: bfloat16 [1024, 1024], P(None, 'tensor'), may hold values from -0.1875 to 0.1875
- value_weight: bfloat16 [1024, 1024], P(None, 'tensor'), may hold values from -0.1875 to 0.1875
- output_weight: bfloat16 [1024, 1024], P('tensor'), may hold values from -0.375 to 0.375
- up_weight: bfloat16 [1024, 2048], P(None, 'tensor'), may hold values from -0.1875 to 0.1875
- up_bias: bfloat16 [2048], P('tensor'), may hold values from -3 to 3
- down_weight: bfloat16 [2048, 1024], P('tensor'), may hold values from -0.25 to 0.25
- first_gain: bfloat16 [1024], replicated, may hold values from 0.5 to 1.5
- first_shift: bfloat16 [1024], replicated, may hold values from -3 to 3
- second_gain: bfloat16 [1024], replicated, may hold values from 0.5 to 1.5
- second_shift: bfloat16 [1024], replicated, may hold values from -3 to 3
- output_bias: bfloat16 [1024], replicated, may hold values from -3 to 3
- down_bias: bfloat16 [1024], replicated, may hold values from -3 to 3
- cotangent: bfloat16 [7680, 1024], P('dp'), may hold values from -12 to 12
Outputs:
- block_out: bfloat16 [7680, 1024], P('dp')
- token_grad: bfloat16 [7680, 1024], P('dp')
- query_grad: float32 [1024, 1024], P(None, 'tensor')
- key_grad: float32 [1024, 1024], P(None, 'tensor')
- value_grad: float32 [1024, 1024], P(None, 'tensor')
- output_grad: float32 [1024, 1024], P('tensor')
- up_grad: float32 [1024, 2048], P(None, 'tensor')
- up_bias_grad: float32 [2048], P('tensor')
- down_grad: float32 [2048, 1024], P('tensor')
- first_gain_grad: float32 [1024], replicated
- first_shift_grad: float32 [1024], replicated
- second_gain_grad: float32 [1024], replicated
- second_shift_grad: float32 [1024], replicated
- output_bias_grad: float32 [1024], replicated
- down_bias_grad: float32 [1024], replicated
All inputs are finite; a program needn't handle non-finite values.
Results may differ from a plain program's by a relative error of at most 0.017.
Values may be sent and summed in bfloat16 or wider, within the bound.
A program may use at most 128 MiB of HBM per device.

v0:
```python
import math

import jax
import jax.numpy as jnp
from jax import lax
from jax.sharding import PartitionSpec as P

DH = 128


EPS = 1e-05


def norm_parts(rows, gain, shift):
    row_mean = jnp.mean(rows, axis=-1, keepdims=True)
    centred = rows - row_mean
    inverse = lax.rsqrt(jnp.mean(centred * centred, axis=-1, keepdims=True) + EPS)
    scaled = centred * inverse
    return (scaled * gain + shift, scaled, inverse)


def norm_back(incoming, scaled, inverse, gain):
    weighted = incoming * gain
    return inverse * (
        weighted
        - jnp.mean(weighted, axis=-1, keepdims=True)
        - scaled * jnp.mean(weighted * scaled, axis=-1, keepdims=True)
    )


def allowed_mask(lengths, count):
    position = jnp.arange(count, dtype=jnp.int32)
    start = (count - lengths)[:, None, None]
    query_pos = position[None, :, None]
    key_pos = position[None, None, :]
    return (key_pos >= start) & (key_pos <= query_pos) | (key_pos == query_pos)


def gelu_exact(values):
    return jax.nn.gelu(values, approximate=False)


def shards(
    tokens,
    lengths,
    query_weight,
    key_weight,
    value_weight,
    output_weight,
    up_weight,
    up_bias,
    down_weight,
    first_gain,
    first_shift,
    second_gain,
    second_shift,
    output_bias,
    down_bias,
    cotangent,
):
    tok_rows = tokens.shape[0]
    series = lengths.shape[0]
    count = tok_rows // series
    heads_here = query_weight.shape[1] // DH
    groups = lax.axis_size("tensor")
    share = tok_rows // groups
    begin = lax.axis_index("tensor") * share
    scale_factor = 1.0 / math.sqrt(DH)
    allowed = allowed_mask(lengths, count)[:, None]

    def share_rows(array):
        return lax.dynamic_slice_in_dim(array, begin, share, 0)

    def to_heads(array):
        return array.reshape(series, count, heads_here, DH)

    def masked_scores(query_four, key_four):
        raw = (
            jnp.einsum("sqhd,skhd->shqk", query_four, key_four, preferred_element_type=jnp.float32)
            * scale_factor
        )
        return jnp.where(allowed, raw, -1e30)

    inputs = tokens.astype(jnp.float32)
    gain_one = first_gain.astype(jnp.float32)
    gain_two = second_gain.astype(jnp.float32)
    first_normed, first_scaled, first_inverse = norm_parts(
        inputs, gain_one, first_shift.astype(jnp.float32)
    )
    first_low = first_normed.astype(jnp.bfloat16)
    queries = jnp.dot(first_low, query_weight, preferred_element_type=jnp.float32).astype(
        jnp.bfloat16
    )
    key_rows = jnp.dot(first_low, key_weight, preferred_element_type=jnp.float32).astype(
        jnp.bfloat16
    )
    value_rows = jnp.dot(first_low, value_weight, preferred_element_type=jnp.float32).astype(
        jnp.bfloat16
    )
    query_four = to_heads(queries)
    key_four = to_heads(key_rows)
    value_four = to_heads(value_rows)
    scores = masked_scores(query_four, key_four)
    row_max = jnp.max(scores, axis=-1, keepdims=True)
    numerator = jnp.exp(scores - row_max)
    row_total = jnp.sum(numerator, axis=-1, keepdims=True)
    log_total = row_max + jnp.log(row_total)
    probs_low = (numerator / row_total).astype(jnp.bfloat16)
    heads_out = jnp.einsum(
        "shqk,skhd->sqhd", probs_low, value_four, preferred_element_type=jnp.float32
    )
    heads_low = heads_out.astype(jnp.bfloat16).reshape(tok_rows, heads_here * DH)
    attn_part = jnp.dot(heads_low, output_weight, preferred_element_type=jnp.float32)
    bias_attn = output_bias.astype(jnp.float32)
    bias_down = down_bias.astype(jnp.float32)
    grad_output = cotangent.astype(jnp.float32)
    attn_share = lax.psum_scatter(attn_part, "tensor", scatter_dimension=0, tiled=True)
    residual_share = share_rows(inputs) + attn_share + bias_attn
    second_share, second_scaled, second_inverse = norm_parts(
        residual_share, gain_two, second_shift.astype(jnp.float32)
    )
    second_low = lax.all_gather(second_share.astype(jnp.bfloat16), "tensor", axis=0, tiled=True)
    up_pre = jnp.dot(second_low, up_weight, preferred_element_type=jnp.float32) + up_bias.astype(
        jnp.float32
    )
    activated, gelu_pull = jax.vjp(gelu_exact, up_pre)
    activated = activated.astype(jnp.bfloat16)
    down_part = jnp.dot(activated, down_weight, preferred_element_type=jnp.float32)
    down_share = lax.psum_scatter(
        down_part.astype(jnp.bfloat16), "tensor", scatter_dimension=0, tiled=True
    ).astype(jnp.float32)
    out_share = (residual_share + down_share + bias_down).astype(jnp.bfloat16)
    block_out = lax.all_gather(out_share, "tensor", axis=0, tiled=True)
    down_bias_part = jnp.sum(share_rows(grad_output), axis=0)
    down_grad = jnp.einsum("tf,td->fd", activated, cotangent, preferred_element_type=jnp.float32)
    activated_grad = jnp.einsum(
        "td,fd->tf", cotangent, down_weight, preferred_element_type=jnp.float32
    )
    up_grad_pre = gelu_pull(activated_grad)[0].astype(jnp.bfloat16)
    up_bias_grad = jnp.sum(up_grad_pre.astype(jnp.float32), axis=0)
    up_grad = jnp.einsum("td,tf->df", second_low, up_grad_pre, preferred_element_type=jnp.float32)
    second_part = jnp.einsum(
        "tf,df->td", up_grad_pre, up_weight, preferred_element_type=jnp.float32
    )
    second_grad_share = lax.psum_scatter(second_part, "tensor", scatter_dimension=0, tiled=True)
    residual_share_grad = share_rows(grad_output) + norm_back(
        second_grad_share, second_scaled, second_inverse, gain_two
    )
    second_gain_part = jnp.sum(second_grad_share * second_scaled, axis=0)
    second_shift_part = jnp.sum(second_grad_share, axis=0)
    output_bias_part = jnp.sum(residual_share_grad, axis=0)
    residual_low = lax.all_gather(
        residual_share_grad.astype(jnp.bfloat16), "tensor", axis=0, tiled=True
    )
    output_grad = jnp.einsum(
        "tc,td->cd", heads_low, residual_low, preferred_element_type=jnp.float32
    )
    heads_grad = jnp.einsum(
        "td,cd->tc", residual_low, output_weight, preferred_element_type=jnp.float32
    )
    heads_grad_four = to_heads(heads_grad.astype(jnp.bfloat16))
    probs_again = jnp.exp(masked_scores(query_four, key_four) - log_total)
    value_rows_grad = jnp.einsum(
        "shqk,sqhd->skhd", probs_low, heads_grad_four, preferred_element_type=jnp.float32
    ).astype(jnp.bfloat16)
    probs_grad = jnp.einsum(
        "sqhd,skhd->shqk", heads_grad_four, value_four, preferred_element_type=jnp.float32
    )
    inner_sum = jnp.sum(probs_again * probs_grad, axis=-1, keepdims=True)
    scores_grad = (probs_again * (probs_grad - inner_sum)).astype(jnp.bfloat16)
    queries_grad = (
        (
            jnp.einsum("shqk,skhd->sqhd", scores_grad, key_four, preferred_element_type=jnp.float32)
            * scale_factor
        )
        .astype(jnp.bfloat16)
        .reshape(tok_rows, heads_here * DH)
    )
    key_rows_grad = (
        (
            jnp.einsum(
                "shqk,sqhd->skhd", scores_grad, query_four, preferred_element_type=jnp.float32
            )
            * scale_factor
        )
        .astype(jnp.bfloat16)
        .reshape(tok_rows, heads_here * DH)
    )
    value_rows_grad = value_rows_grad.reshape(tok_rows, heads_here * DH)
    query_grad = jnp.einsum(
        "td,tc->dc", first_low, queries_grad, preferred_element_type=jnp.float32
    )
    key_grad = jnp.einsum("td,tc->dc", first_low, key_rows_grad, preferred_element_type=jnp.float32)
    value_grad = jnp.einsum(
        "td,tc->dc", first_low, value_rows_grad, preferred_element_type=jnp.float32
    )
    first_part = (
        jnp.einsum("tc,dc->td", queries_grad, query_weight, preferred_element_type=jnp.float32)
        + jnp.einsum("tc,dc->td", key_rows_grad, key_weight, preferred_element_type=jnp.float32)
        + jnp.einsum("tc,dc->td", value_rows_grad, value_weight, preferred_element_type=jnp.float32)
    )
    first_grad_share = lax.psum_scatter(
        first_part.astype(jnp.bfloat16), "tensor", scatter_dimension=0, tiled=True
    ).astype(jnp.float32)
    scaled_share = share_rows(first_scaled)
    token_share = residual_share_grad + norm_back(
        first_grad_share, scaled_share, share_rows(first_inverse), gain_one
    )
    token_grad = lax.all_gather(token_share.astype(jnp.bfloat16), "tensor", axis=0, tiled=True)
    first_gain_part = jnp.sum(first_grad_share * scaled_share, axis=0)
    first_shift_part = jnp.sum(first_grad_share, axis=0)
    query_grad, key_grad, value_grad, output_grad, up_grad, up_bias_grad, down_grad = (
        lax.psum(query_grad.astype(jnp.bfloat16), "dp").astype(jnp.float32),
        lax.psum(key_grad.astype(jnp.bfloat16), "dp").astype(jnp.float32),
        lax.psum(value_grad.astype(jnp.bfloat16), "dp").astype(jnp.float32),
        lax.psum(output_grad.astype(jnp.bfloat16), "dp").astype(jnp.float32),
        lax.psum(up_grad.astype(jnp.bfloat16), "dp").astype(jnp.float32),
        lax.psum(up_bias_grad.astype(jnp.bfloat16), "dp").astype(jnp.float32),
        lax.psum(down_grad.astype(jnp.bfloat16), "dp").astype(jnp.float32),
    )
    (
        first_gain_grad,
        first_shift_grad,
        second_gain_grad,
        second_shift_grad,
        output_bias_grad,
        down_bias_grad,
    ) = lax.psum(
        (
            first_gain_part,
            first_shift_part,
            second_gain_part,
            second_shift_part,
            output_bias_part,
            down_bias_part,
        ),
        ("dp", "tensor"),
    )
    return (
        block_out,
        token_grad,
        query_grad,
        key_grad,
        value_grad,
        output_grad,
        up_grad,
        up_bias_grad,
        down_grad,
        first_gain_grad,
        first_shift_grad,
        second_gain_grad,
        second_shift_grad,
        output_bias_grad,
        down_bias_grad,
    )


def solution(mesh):
    return jax.shard_map(
        shards,
        mesh=mesh,
        in_specs=(
            P("dp", None),
            P("dp"),
            P(None, "tensor"),
            P(None, "tensor"),
            P(None, "tensor"),
            P("tensor", None),
            P(None, "tensor"),
            P("tensor"),
            P("tensor", None),
            P(),
            P(),
            P(),
            P(),
            P(),
            P(),
            P("dp", None),
        ),
        out_specs=(
            P("dp", None),
            P("dp", None),
            P(None, "tensor"),
            P(None, "tensor"),
            P(None, "tensor"),
            P("tensor", None),
            P(None, "tensor"),
            P("tensor"),
            P("tensor", None),
            P(),
            P(),
            P(),
            P(),
            P(),
            P(),
        ),
        check_vma=False,
    )
```

profile of v0, /device:TPU:0, one launch (start us, length us, event | category | flops | bytes accessed | tf_op | source)
XLA Modules:
  0.0 483.9 jit_solution(16152357230781706024)
XLA Ops:
  10.1 2.7 subtract_multiply_fusion
  16.7 3.3 convolution_convert_fusion.10
  22.0 3.1 convolution_convert_fusion.12
  30.9 2.6 fusion.32
  36.0 43.2 %reduce-scatter.5.cloned.1.call-done = f32[240,1024]{1,0:T(8,128)} async-done(((f32[960,1024]{1,0:T(8,128)}), f32[240,1024]{1,0:T(8,128)}) %reduce-scatter.5.cloned.1.call-update) | async-done | bytes 983056 | tf_op jit(solution)/shard_map/reduce_scatter | solution.py:117
  82.3 21.9 %all-gather.5.cloned.1.call-done = bf16[960,1024]{1,0:T(8,128)(2,1)} async-done(((bf16[240,1024]{1,0:T(8,128)(2,1)}), bf16[960,1024]{1,0:T(8,128)(2,1)}) %all-gather.5.cloned.1.call-update) | async-done | bytes 1966096 | tf_op jit(solution)/shard_map/all_gather | solution.py:122
  104.3 3.1 fusion.56
  107.4 6.7 %fusion.52 = (bf16[512]{0:T(512)(128)(2,1)S(1)}, bf16[960,512]{1,0:T(8,128)(2,1)S(1)}, f32[960,512]{1,0:T(8,128)}) fusion(f32[960,512]{1,0:T(8,128)S(1)} %fusion.56, f32[512]{0:T(512)S(1)} %convert_element_type.157, bf16[960,1024]{1,0:T(8,128)(2,1)S(1)} %copy-done.33, bf16[512,1024]{1,0:T(8,128)(2,1)S(1)} %copy-done), kind=kOutput, calls=%fused_computation.116 | convolution fusion | flops 1043004928 | bytes 7932928 | tf_op jit(solution)/shard_map/td,fd->tf/dot_general | solution.py:136
  114.1 3.1 fusion.57
  117.5 2.6 multiply_convert_fusion
  121.1 2.5 convolution_convert_fusion
  124.2 36.1 %reduce-scatter.9.cloned.1.call-done = f32[240,1024]{1,0:T(8,128)} async-done(((f32[960,1024]{1,0:T(8,128)}), f32[240,1024]{1,0:T(8,128)}) %reduce-scatter.9.cloned.1.call-update) | async-done | bytes 983056 | tf_op jit(solution)/shard_map/reduce_scatter | solution.py:145
  162.1 31.9 %reduce-scatter.7.cloned.1.call-done = bf16[240,1024]{1,0:T(8,128)(2,1)} async-done(((bf16[960,1024]{1,0:T(8,128)(2,1)}), bf16[240,1024]{1,0:T(8,128)(2,1)}) %reduce-scatter.7.cloned.1.call-update) | async-done | bytes 491536 | tf_op jit(solution)/shard_map/reduce_scatter | solution.py:129
  194.0 2.5 fusion.51
  197.5 21.9 %all-gather.9.cloned.1.call-done = bf16[960,1024]{1,0:T(8,128)(2,1)} async-done(((bf16[240,1024]{1,0:T(8,128)(2,1)}), bf16[960,1024]{1,0:T(8,128)(2,1)}) %all-gather.9.cloned.1.call-update) | async-done | bytes 1966096 | tf_op jit(solution)/shard_map/all_gather | solution.py:152
  219.4 3.0 convolution_convert_fusion.9
  233.0 4.2 convolution_convert_fusion.1
  245.9 16.9 %reduce-scatter.11.cloned.1.call-done = bf16[240,1024]{1,0:T(8,128)(2,1)} async-done(((bf16[960,1024]{1,0:T(8,128)(2,1)}), bf16[240,1024]{1,0:T(8,128)(2,1)}) %reduce-scatter.11.cloned.1.call-update) | async-done | bytes 491536 | tf_op jit(solution)/shard_map/reduce_scatter | solution.py:202
  264.5 2.4 fusion.19
  267.0 21.3 %psum.96 = bf16[512]{0:T(512)(128)(2,1)S(1)} all-reduce(bf16[512]{0:T(512)(128)(2,1)S(1)} %get-tuple-element.37), channel_id=1, replica_groups=mesh['dp'=8,'tensor'=4] {'dp'}, use_global_device_ids=true, to_apply=%region_21.22 | all-reduce | flops 512 | bytes 2048 | tf_op jit(solution)/shard_map/psum | solution.py:218
  288.9 41.7 %all-reduce = (f32[1024]{0:T(1024)}, f32[1024]{0:T(1024)}, f32[1024]{0:T(1024)}, f32[1024]{0:T(1024)}, f32[1024]{0:T(1024)}, /*index=5*/f32[1024]{0:T(1024)}) all-reduce(f32[1024]{0:T(1024)S(1)} %get-tuple-element.15, f32[1024]{0:T(1024)S(1)} %get-tuple-element.22, ...), channel_id=1, replica_groups=mesh['dp'=8,'tensor'=4] {'dp','tensor'}, use_global_device_ids=true, to_apply=%region_24.25 | all-reduce | flops 6144 | bytes 49152 | tf_op jit(solution)/shard_map/psum | solution.py:228
  330.6 120.6 %all-reduce.4.cloned.1.call-done = (bf16[1024,256]{1,0:T(8,128)(2,1)}, bf16[1024,256]{1,0:T(8,128)(2,1)}, bf16[1024,256]{1,0:T(8,128)(2,1)}, bf16[256,1024]{1,0:...) async-done(((bf16[1024,256]{1,0:T(8,128)(2,1)}, bf16[1024,256]{1,0:T(8,128)(2,1)}, bf16[1024,256]{1,0:T(8,128)(2,1)}, bf16[256,1024]{1,0:T(8,128)(2,1)}, ...) | async-done | bytes 4194320 | tf_op jit(solution)/shard_map/psum | solution.py:213
  451.1 2.9 convert_element_type.186
  459.9 14.0 %all-gather.11.cloned.1.call-done = bf16[960,1024]{1,0:T(8,128)(2,1)} async-done(((bf16[240,1024]{1,0:T(8,128)(2,1)}), bf16[960,1024]{1,0:T(8,128)(2,1)}) %all-gather.11.cloned.1.call-update) | async-done | bytes 1966096 | tf_op jit(solution)/shard_map/all_gather | solution.py:209
  (174 shorter events, 55.2 us)
Async XLA Ops:
  7.2 100.2 %copy-start = (bf16[512,1024]{1,0:T(8,128)(2,1)S(1)}, bf16[512,1024]{1,0:T(8,128)(2,1)}, u32[]{:S(2)}) copy-start(bf16[512,1024]{1,0:T(8,128)(2,1)} %param.24) | copy-start | bytes 3145732
  7.2 72.0 %reduce-scatter.5.cloned.1.call-start = ((), (), s32[]{:S(2)}) async-start(), calls=%async_computation.4 | async-start | bytes 4915200 | tf_op jit(solution)/shard_map/reduce_scatter | solution.py:117
  10.1 4.0 copy-start.22
  16.7 10.5 %copy-start.6 = (bf16[64,15,2,128]{3,2,1,0:T(2,128)(2,1)}, bf16[64,15,2,128]{3,2,1,0:T(2,128)(2,1)S(1)}, u32[]{:S(2)}) copy-start(bf16[64,15,2,128]{3,2,1,0:T(2,128)(2,1)S(1)} %reshape.181) | copy-start | bytes 1474564
  16.7 5.2 %copy-start.43 = (s32[64]{0:T(128)S(1)}, s32[64]{0:T(128)}, u32[]{:S(2)}) copy-start(s32[64]{0:T(128)} %param.17) | copy-start | bytes 772
  33.5 70.7 %all-gather.5.cloned.1.call-start = ((), (), s32[]{:S(2)}) async-start(), calls=%async_computation.5 | async-start | bytes 2457600 | tf_op jit(solution)/shard_map/all_gather | solution.py:122
  82.3 78.0 %reduce-scatter.9.cloned.1.call-start = ((), (), s32[]{:S(2)}) async-start(), calls=%async_computation.8 | async-start | bytes 4915200 | tf_op jit(solution)/shard_map/reduce_scatter | solution.py:145
  104.3 3.2 copy-start.33
  107.4 6.7 %copy-start.14 = (f32[960,512]{1,0:T(8,128)}, f32[960,512]{1,0:T(8,128)S(1)}, u32[]{:S(2)}) copy-start(f32[960,512]{1,0:T(8,128)S(1)} %fusion.56) | copy-start | bytes 5898244
  107.4 6.7 %copy-start.42 = (bf16[1024,512]{1,0:T(8,128)(2,1)S(1)}, bf16[1024,512]{1,0:T(8,128)(2,1)}, u32[]{:S(2)}) copy-start(bf16[1024,512]{1,0:T(8,128)(2,1)} %param.22) | copy-start | bytes 3145732
  114.1 3.1 copy-start.44
  117.3 76.7 %reduce-scatter.7.cloned.1.call-start = ((), (), s32[]{:S(2)}) async-start(), calls=%async_computation.6 | async-start | bytes 2457600 | tf_op jit(solution)/shard_map/reduce_scatter | solution.py:129
  123.6 95.8 %all-gather.9.cloned.1.call-start = ((), (), s32[]{:S(2)}) async-start(), calls=%async_computation.9 | async-start | bytes 2457600 | tf_op jit(solution)/shard_map/all_gather | solution.py:152
  160.3 33.7 %copy-start.5 = (f32[240,1024]{1,0:T(8,128)S(1)}, f32[240,1024]{1,0:T(8,128)}, u32[]{:S(2)}) copy-start(f32[240,1024]{1,0:T(8,128)} %reduce-scatter.9.cloned.1.call-done) | copy-start | bytes 2949124
  196.5 22.9 %copy-start.20 = (bf16[256,1024]{1,0:T(8,128)(2,1)S(1)}, bf16[256,1024]{1,0:T(8,128)(2,1)}, u32[]{:S(2)}) copy-start(bf16[256,1024]{1,0:T(8,128)(2,1)} %param.21) | copy-start | bytes 1572868
  197.4 65.4 %reduce-scatter.11.cloned.1.call-start = ((), (), s32[]{:S(2)}) async-start(), calls=%async_computation.10 | async-start | bytes 2457600 | tf_op jit(solution)/shard_map/reduce_scatter | solution.py:202
  197.5 26.1 %copy-start.4 = (f32[64,2,15,15]{2,3,1,0:T(8,128)S(1)}, f32[64,2,15,15]{2,3,1,0:T(8,128)}, u32[]{:S(2)}) copy-start(f32[64,2,15,15]{2,3,1,0:T(8,128)} %copy-done.3) | copy-start | bytes 345604
  231.9 57.0 %all-gather.7.cloned.1.call-start = ((), (), s32[]{:S(2)}) async-start(), calls=%async_computation.7 | async-start | bytes 2457600 | tf_op jit(solution)/shard_map/all_gather | solution.py:133
  232.7 218.5 %all-reduce.4.cloned.1.call-start = ((), (), s32[]{:S(2)}) async-start(), calls=%async_computation.12 | async-start | bytes 8388608 | tf_op jit(solution)/shard_map/psum | solution.py:213
  232.9 4.3 copy-start.41
  233.0 4.3 copy-start.45
  245.7 228.1 %all-gather.11.cloned.1.call-start = ((), (), s32[]{:S(2)}) async-start(), calls=%async_computation.11 | async-start | bytes 2457600 | tf_op jit(solution)/shard_map/all_gather | solution.py:209
  457.7 16.1 %copy-start.11 = (bf16[960,1024]{1,0:T(8,128)(2,1)S(1)}, bf16[960,1024]{1,0:T(8,128)(2,1)}, u32[]{:S(2)}) copy-start(bf16[960,1024]{1,0:T(8,128)(2,1)} %all-gather.7.cloned.1.call-done) | copy-start | bytes 5898244
  473.9 3.5 copy-start.1
  (31 other events, 53.0 us)
Sparse Core Ops, SparseCore 0:
  33.6 45.5 reduce-scatter.4
  82.4 21.8 all-gather.4
  117.4 42.8 reduce-scatter.8
  163.3 30.6 reduce-scatter.6
  197.5 21.8 all-gather.8
  232.0 30.6 reduce-scatter.10
  264.3 21.8 all-gather.6
  291.8 159.3 all-reduce.3
  453.3 20.5 all-gather.10
where the time goes:
time: 485 us; the launch traced here: 484 us
  waiting for transfers between devices  307 us (63%)
  blocking collectives  63 us (13%)
  matrix products  48.5 us (10%)
  other arithmetic  33 us (7%)
  local copies, waits for them, and re-layouts  16.9 us (3%)
  between operations  14.5 us (3%)
    psum x1, waiting for transfers between devices, shards(): lax.psum(query_grad.astype(jnp.bfloat16), 'dp').astype(jnp.float32)  121 us
    reduce_scatter x1, waiting for transfers between devices, shards(): lax.psum_scatter(attn_part, 'tensor', scatter_dimension=0, tiled=True)  43.2 us
    psum x1, blocking collectives, shards(): lax.psum((first_gain_part, first_shift_part, second_gain_part, second_shi...  41.7 us
    reduce_scatter x1, waiting for transfers between devices, shards(): lax.psum_scatter(second_part, 'tensor', scatter_dimension=0, tiled=True)  36.1 us
    reduce_scatter x1, waiting for transfers between devices, shards(): lax.psum_scatter(down_part.astype(jnp.bfloat16), 'tensor', scatter_dimens...  31.9 us
    all_gather x1, waiting for transfers between devices, shards(): lax.all_gather(second_share.astype(jnp.bfloat16), 'tensor', axis=0, tiled...  21.9 us
    all_gather x1, waiting for transfers between devices, shards(): lax.all_gather(residual_share_grad.astype(jnp.bfloat16), 'tensor', axis=0...  21.9 us
    psum x1, blocking collectives, shards(): lax.psum(up_bias_grad.astype(jnp.bfloat16), 'dp').astype(jnp.float32)  21.3 us
  transfers between devices with their start and end apart: 9, of which 8 were waited for; matrix products, arithmetic and copies ran while one was open for 7% of the time, Pallas kernels for 0%

commit v1 on v0

--- a/solution.py
+++ b/solution.py
@@ -1,8 +1,11 @@
+import functools
 import math
 
 import jax
 import jax.numpy as jnp
 from jax import lax
+from jax.experimental import pallas as pl
+from jax.experimental.pallas import tpu as pltpu
 from jax.sharding import PartitionSpec as P
 
 DH = 128
@@ -40,7 +43,7 @@
     return jax.nn.gelu(values, approximate=False)
 
 
-def shards(
+def plain_shards(
     tokens,
     lengths,
     query_weight,
@@ -255,9 +258,772 @@
     )
 
 
+F32 = jnp.float32
+BF16 = jnp.bfloat16
+MESH = pl.DeviceIdType.MESH
+SUB = 80
+N_SEMS = 128
+
+
+def dot(a, b):
+    return jnp.dot(a, b, preferred_element_type=F32)
+
+
+def dot_nt(a, b):
+    return lax.dot_general(a, b, (((1,), (1,)), ((), ())), preferred_element_type=F32)
+
+
+def dot_tn(a, b):
+    return lax.dot_general(a, b, (((0,), (0,)), ((), ())), preferred_element_type=F32)
+
+
+def span(start, size):
+    return pl.ds(pl.multiple_of(start, 16), size)
+
+
+def lanes(start, size):
+    return pl.ds(pl.multiple_of(start, 128), size)
+
+
+class Links:
+    def __init__(self, sends, recvs, anyone):
+        self.sends, self.recvs, self.anyone = sends, recvs, anyone
+        self.used = 0
+
+    def take(self, count=1):
+        first = self.used
+        self.used += count
+        assert self.used <= N_SEMS
+        return first
+
+    def copy(self, src, dst, index, device):
+        return pltpu.make_async_remote_copy(
+            src_ref=src,
+            dst_ref=dst,
+            send_sem=self.sends.at[index],
+            recv_sem=self.recvs.at[index],
+            device_id=device,
+            device_id_type=MESH,
+        )
+
+    def got(self, dst, index):
+        self.copy(dst, dst, index, self.anyone).wait_recv()
+
+    def sent(self, src, index):
+        self.copy(src, src, index, self.anyone).wait_send()
+
+
+def layer_kernel(
+    count,
+    tokens,
+    lengths,
+    query_weight,
+    key_weight,
+    value_weight,
+    output_weight,
+    up_weight,
+    up_bias,
+    down_weight,
+    first_gain,
+    first_shift,
+    second_gain,
+    second_shift,
+    output_bias,
+    down_bias,
+    cotangent,
+    block_out,
+    token_grad,
+    down_out,
+    up_out,
+    output_out,
+    qkv_out,
+    vec_out,
+    first_low,
+    queries,
+    key_rows,
+    value_rows,
+    probs,
+    heads_own,
+    heads_full,
+    wo_all,
+    residual,
+    second_low,
+    act,
+    ugp,
+    mail,
+    residual_grad,
+    residual_low,
+    dqkv,
+    g_down,
+    g_up,
+    g_output,
+    g_qkv,
+    rx_down,
+    rx_up,
+    rx_output,
+    rx_qkv,
+    rz_down,
+    rz_up,
+    rz_output,
+    rz_qkv,
+    rm_down,
+    rm_up,
+    rm_output,
+    rm_qkv,
+    t_down,
+    t_up,
+    t_output,
+    t_qkv,
+    vec,
+    vec_sib,
+    vec_parts,
+    vec_sum,
+    vec_all,
+    sends,
+    recvs,
+    local_sems,
+):
+    n_rows, width = tokens.shape
+    half = n_rows // 2
+    tile = 16 * count
+    n_tiles = n_rows // tile
+    half_tiles = n_tiles // 2
+    heads_here = query_weight.shape[1] // DH
+    cols = heads_here * DH
+    hidden = up_weight.shape[1]
+    scale_factor = 1.0 / math.sqrt(DH)
+
+    dp = lax.axis_index("dp")
+    t = lax.axis_index("tensor")
+    x = dp % 2
+    z = dp // 2
+    c = t % 2
+    t_sib = t + 1 - 2 * c
+    t_opp = (t + 2) % 4
+    t_diag = (t_sib + 2) % 4
+    sib = (dp, t_sib)
+    opp = (dp, t_opp)
+    diag = (dp, t_diag)
+    xp = (dp + 1 - 2 * x, t)
+    adj = (dp + 2 - 4 * (z % 2), t)
+    mid = ((3 - z) * 2 + x, t)
+    is_mid = jnp.logical_or(z == 1, z == 2)
+    is_end = jnp.logical_or(z == 0, z == 3)
+    dp_peers = [((dp + k) % 8, t) for k in range(1, 8)]
+    links = Links(sends, recvs, sib)
+
+    barrier = pltpu.get_barrier_semaphore()
+    for peer in [sib, opp, diag] + dp_peers:
+        pl.semaphore_signal(barrier, inc=1, device_id=peer, device_id_type=MESH)
+
+    def row(ref):
+        return ref[...].astype(F32).reshape(1, ref.shape[0])
+
+    own_start = c * half
+    sib_start = (1 - c) * half
+
+    def first_norm(i, _):
+        rows = span(i * SUB, SUB)
+        v = tokens[rows, :].astype(F32)
+        e = v - jnp.mean(v, axis=-1, keepdims=True)
+        r = lax.rsqrt(jnp.mean(e * e, axis=-1, keepdims=True) + EPS)
+        first_low[rows, :] = (e * r * row(first_gain) + row(first_shift)).astype(BF16)
+        return 0
+
+    lax.fori_loop(0, n_rows // SUB, first_norm, 0)
+
+    pl.semaphore_wait(barrier, 10)
+
+    wo_rows = [span(v * cols, cols) for v in (t, t_sib, t_opp, t_diag)]
+    wo_all[wo_rows[0], :] = output_weight[...]
+    i_wo = links.take(3)
+    wo_sends = [
+        links.copy(output_weight, wo_all.at[wo_rows[0], :], i_wo, opp),
+        links.copy(output_weight, wo_all.at[wo_rows[0], :], i_wo + 1, sib),
+        links.copy(wo_all.at[wo_rows[2], :], wo_all.at[wo_rows[2], :], i_wo + 2, sib),
+    ]
+    wo_sends[0].start()
+    wo_sends[1].start()
+
+    def allowed_of(number):
+        def series_of(index):
+            return jnp.floor((index + 0.5) * (1.0 / count))
+
+        row_at = lax.broadcasted_iota(jnp.int32, (tile, 1), 0).astype(F32)
+        col_at = lax.broadcasted_iota(jnp.int32, (1, tile), 1).astype(F32)
+        row_series, col_series = series_of(row_at), series_of(col_at)
+        n_series = lengths.shape[0]
+        which = lax.broadcasted_iota(jnp.int32, (n_series, tile), 0).astype(F32)
+        here = (which == col_series + (number * 16).astype(F32)).astype(BF16)
+        all_lengths = jnp.broadcast_to(
+            lengths[...].astype(F32).reshape(1, n_series), (8, n_series)
+        ).astype(BF16)
+        length = dot(all_lengths, here)[0:1, :]
+        live = (col_at - count * col_series) >= (count - length)
+        same = row_series == col_series
+        seen = jnp.logical_and(live, col_at <= row_at)
+        return jnp.logical_and(same, jnp.logical_or(seen, col_at == row_at))
+
+    i_heads = links.take(3 * half_tiles)
+
+    def head_slot(j):
+        return span(j * tile, tile)
+
+    def attend(i, _):
+        h, j = i % 2, i // 2
+        number = h * half_tiles + j
+        rows = span(number * tile, tile)
+        normed = first_low[rows, :]
+        q = dot(normed, query_weight[...]).astype(BF16)
+        k = dot(normed, key_weight[...]).astype(BF16)
+        v = dot(normed, value_weight[...]).astype(BF16)
+        queries[rows, :] = q
+        key_rows[rows, :] = k
+        value_rows[rows, :] = v
+        allowed = allowed_of(number)
+        for head in range(heads_here):
+            at = slice(head * DH, (head + 1) * DH)
+            scores = jnp.where(allowed, dot_nt(q[:, at], k[:, at]) * scale_factor, -1e30)
+            numerator = jnp.exp(scores - jnp.max(scores, axis=-1, keepdims=True))
+            share = numerator / jnp.sum(numerator, axis=-1, keepdims=True)
+            probs[number * heads_here + head] = share
+            heads_own[rows, at] = dot(share.astype(BF16), v[:, at]).astype(BF16)
+        slot = heads_full.at[head_slot(j), lanes(t * cols, cols)]
+
+        @pl.when(h == c)
+        def _():
+            heads_full[head_slot(j), lanes(t * cols, cols)] = heads_own[rows, :]
+            links.copy(heads_own.at[rows, :], slot, i_heads + j, opp).start()
+
+        @pl.when(h != c)
+        def _():
+            links.copy(heads_own.at[rows, :], slot, i_heads + half_tiles + j, sib).start()
+            links.copy(heads_own.at[rows, :], slot, i_heads + 2 * half_tiles + j, diag).start()
+
+        return 0
+
+    lax.fori_loop(0, n_tiles, attend, 0)
+
+    links.got(wo_all.at[wo_rows[2], :], i_wo)
+    wo_sends[2].start()
+    links.got(wo_all.at[wo_rows[1], :], i_wo + 1)
+    links.got(wo_all.at[wo_rows[3], :], i_wo + 2)
+
+    i_second = links.take(half_tiles)
+
+    def residual_stats(rows):
+        v = residual[rows, :]
+        e = v - jnp.mean(v, axis=-1, keepdims=True)
+        r = lax.rsqrt(jnp.mean(e * e, axis=-1, keepdims=True) + EPS)
+        return e * r, r
+
+    def project(j, _):
+        here = head_slot(j)
+        for n, who in enumerate((t_opp, t_sib, t_diag)):
+            links.got(heads_full.at[here, lanes(who * cols, cols)], i_heads + n * half_tiles + j)
+        rows = span(own_start + j * tile, tile)
+        residual[here, :] = (
+            tokens[rows, :].astype(F32) + dot(heads_full[here, :], wo_all[...]) + row(output_bias)
+        )
+
+        def second_norm(s, _):
+            local = span(j * tile + s * SUB, SUB)
+            xhat, _r = residual_stats(local)
+            second_low[span(own_start + j * tile + s * SUB, SUB), :] = (
+                xhat * row(second_gain) + row(second_shift)
+            ).astype(BF16)
+            return 0
+
+        lax.fori_loop(0, tile // SUB, second_norm, 0)
+        links.copy(second_low.at[rows, :], second_low.at[rows, :], i_second + j, sib).start()
+        return 0
+
+    lax.fori_loop(0, half_tiles, project, 0)
+
+    vec[...] = jnp.zeros_like(vec)
+
+    def in_turn(i):
+        return jnp.where(i % 2 == 0, own_start, sib_start) + (i // 2) * tile
+
+    def feed(i, _):
+        rows = span(in_turn(i), tile)
+
+        @pl.when(i % 2 == 1)
+        def _():
+            links.got(second_low.at[rows, :], i_second + i // 2)
+
+        u = dot(second_low[rows, :], up_weight[...]) + row(up_bias)
+        big = 0.5 * (1.0 + lax.erf(u * (1.0 / math.sqrt(2.0))))
+        act[rows, :] = (u * big).astype(BF16)
+        slope = big + u * (jnp.exp(-0.5 * u * u) * (1.0 / math.sqrt(2.0 * math.pi)))
+        grad = (dot_nt(cotangent[rows, :], down_weight[...]) * slope).astype(BF16)
+        ugp[rows, :] = grad
+        vec[6:7, 0:hidden] += jnp.sum(grad.astype(F32), axis=0, keepdims=True)
+        return 0
+
+    lax.fori_loop(0, n_tiles, feed, 0)
+
+    class Sum:
+        def __init__(self, grads, rx, rz, rm, total, out):
+            self.grads, self.rx, self.rz, self.rm, self.total, self.out = (
+                grads, rx, rz, rm, total, out,
+            )
+            self.size = grads.shape[0] // 2
+            self.mine = span(x * self.size, self.size)
+            self.other = span((1 - x) * self.size, self.size)
+            self.index = links.take(5)
+
+        def add(self, into, take):
+            step = 32
+
+            def body(i, _):
+                at = span(i * step, step)
+                own = span(x * self.size + i * step, step)
+                into[at if into is self.total else own, :] = (
+                    self.grads[own, :].astype(F32) + take[at, :].astype(F32)
+                ).astype(BF16)
+                return 0
+
+            lax.fori_loop(0, self.size // step, body, 0)
+
+        def to_x(self):
+            links.copy(self.grads.at[self.other, :], self.rx, self.index, xp).start()
+
+        def add_x(self):
+            links.got(self.rx, self.index)
+            self.add(self.grads, self.rx)
+
+            @pl.when(is_end)
+            def _():
+                links.copy(self.grads.at[self.mine, :], self.rz, self.index + 1, adj).start()
+
+        def add_z(self):
+            @pl.when(is_mid)
+            def _():
+                links.got(self.rz, self.index + 1)
+                self.add(self.grads, self.rz)
+                links.copy(self.grads.at[self.mine, :], self.rm, self.index + 2, mid).start()
+
+        def finish_z(self):
+            @pl.when(is_mid)
+            def _():
+                links.got(self.rm, self.index + 2)
+                self.add(self.total, self.rm)
+                links.copy(self.total, self.total, self.index + 3, adj).start()
+                links.copy(self.total, self.out.at[self.mine, :], self.index + 4, xp).start()
+
+        def back_x(self):
+            @pl.when(is_end)
+            def _():
+                links.got(self.total, self.index + 3)
+                links.copy(self.total, self.out.at[self.mine, :], self.index + 4, xp).start()
+
+        def write(self, sem):
+            return pltpu.make_async_copy(self.total, self.out.at[self.mine, :], sem)
+
+        def end(self):
+            links.got(self.out.at[self.other, :], self.index + 4)
+            links.sent(self.grads.at[self.other, :], self.index)
+
+            @pl.when(is_end)
+            def _():
+                links.sent(self.grads.at[self.mine, :], self.index + 1)
+
+            @pl.when(is_mid)
+            def _():
+                links.sent(self.grads.at[self.mine, :], self.index + 2)
+                links.sent(self.total, self.index + 3)
+
+            links.sent(self.total, self.index + 4)
+
+    sum_down = Sum(g_down, rx_down, rz_down, rm_down, t_down, down_out)
+    sum_up = Sum(g_up, rx_up, rz_up, rm_up, t_up, up_out)
+    sum_output = Sum(g_output, rx_output, rz_output, rm_output, t_output, output_out)
+    sum_qkv = Sum(g_qkv, rx_qkv, rz_qkv, rm_qkv, t_qkv, qkv_out)
+
+    def down_grads(i, _):
+        at = lanes(i * 256, 256)
+        g_down[span(i * 256, 256), :] = dot_tn(act[:, at], cotangent[...]).astype(BF16)
+        return 0
+
+    lax.fori_loop(0, hidden // 256, down_grads, 0)
+    sum_down.to_x()
+
+    class RowSum:
+        def __init__(self, number, part):
+            self.snd, self.r1, self.cs, self.r2 = (mail.at[4 * number + n] for n in range(4))
+            self.part = part
+            self.index = links.take(2 * half_tiles)
+
+        def start(self):
+            def far(j, _):
+                here = head_slot(j)
+                self.snd[here, :] = self.part(span(sib_start + j * tile, tile)).astype(BF16)
+                links.copy(self.snd.at[here, :], self.r1.at[here, :], self.index + j, sib).start()
+                return 0
+
+            def near(j, _):
+                here = head_slot(j)
+                mine = self.part(span(own_start + j * tile, tile))
+                links.got(self.r1.at[here, :], self.index + j)
+                self.cs[here, :] = (mine + self.r1[here, :].astype(F32)).astype(BF16)
+                links.copy(
+                    self.cs.at[here, :], self.r2.at[here, :], self.index + half_tiles + j, opp
+                ).start()
+                return 0
+
+            lax.fori_loop(0, half_tiles, far, 0)
+            lax.fori_loop(0, half_tiles, near, 0)
+
+        def wait(self, j):
+            links.got(self.r2.at[head_slot(j), :], self.index + half_tiles + j)
+
+        def rows(self, local):
+            return self.cs[local, :].astype(F32) + self.r2[local, :].astype(F32)
+
+        def end(self):
+            def body(j, _):
+                here = head_slot(j)
+                links.sent(self.snd.at[here, :], self.index + j)
+                links.sent(self.cs.at[here, :], self.index + half_tiles + j)
+                return 0
+
+            lax.fori_loop(0, half_tiles, body, 0)
+
+    second_sum = RowSum(0, lambda rows: dot_nt(ugp[rows, :], up_weight[...]))
+    second_sum.start()
+
+    def up_grads(i, _):
+        at = lanes(i * 256, 256)
+        g_up[span(i * 256, 256), :] = dot_tn(second_low[:, at], ugp[...]).astype(BF16)
+        return 0
+
+    lax.fori_loop(0, width // 256, up_grads, 0)
+    sum_up.to_x()
+
+    out_sum = RowSum(1, lambda rows: dot(act[rows, :], down_weight[...]))
+    out_sum.start()
+
+    i_back = links.take(half_tiles)
+
+    def add_to(at, value):
+        vec[at : at + 1, :] += jnp.sum(value, axis=0, keepdims=True)
+
+    def norm_back(incoming, xhat, r, gain):
+        weighted = incoming * gain
+        return r * (
+            weighted
+            - jnp.mean(weighted, axis=-1, keepdims=True)
+            - xhat * jnp.mean(weighted * xhat, axis=-1, keepdims=True)
+        )
+
+    def second_back(j, _):
+        second_sum.wait(j)
+
+        def body(s, _):
+            local = span(j * tile + s * SUB, SUB)
+            rows = span(own_start + j * tile + s * SUB, SUB)
+            incoming = second_sum.rows(local)
+            xhat, r = residual_stats(local)
+            given = cotangent[rows, :].astype(F32)
+            grad = given + norm_back(incoming, xhat, r, row(second_gain))
+            residual_grad[local, :] = grad
+            residual_low[rows, :] = grad.astype(BF16)
+            add_to(2, incoming * xhat)
+            add_to(3, incoming)
+            add_to(4, grad)
+            add_to(5, given)
+            return 0
+
+        lax.fori_loop(0, tile // SUB, body, 0)
+        rows = span(own_start + j * tile, tile)
+        links.copy(residual_low.at[rows, :], residual_low.at[rows, :], i_back + j, sib).start()
+        return 0
+
+    lax.fori_loop(0, half_tiles, second_back, 0)
+
+    sum_down.add_x()
+    sum_up.add_x()
+
+    def attend_back(i, _):
+        start = in_turn(i)
+        rows = span(start, tile)
+        number = start // tile
+
+        @pl.when(i % 2 == 1)
+        def _():
+            links.got(residual_low.at[rows, :], i_back + i // 2)
+
+        grads = dot_nt(residual_low[rows, :], output_weight[...]).astype(BF16)
+        for head in range(heads_here):
+            at = slice(head * DH, (head + 1) * DH)
+            share = probs[number * heads_here + head]
+            q, k, v = queries[rows, at], key_rows[rows, at], value_rows[rows, at]
+            share_grad = dot_nt(grads[:, at], v)
+            inner = jnp.sum(share * share_grad, axis=-1, keepdims=True)
+            scores_grad = (share * (share_grad - inner)).astype(BF16)
+            dqkv[rows, head * DH : (head + 1) * DH] = (
+                dot(scores_grad, k) * scale_factor
+            ).astype(BF16)
+            dqkv[rows, cols + head * DH : cols + (head + 1) * DH] = (
+                dot_tn(scores_grad, q) * scale_factor
+            ).astype(BF16)
+            dqkv[rows, 2 * cols + head * DH : 2 * cols + (head + 1) * DH] = dot_tn(
+                share.astype(BF16), grads[:, at]
+            ).astype(BF16)
+        return 0
+
+    lax.fori_loop(0, n_tiles, attend_back, 0)
+
+    sum_down.add_z()
+
+    first_sum = RowSum(
+        2,
+        lambda rows: dot_nt(dqkv[rows, 0:cols], query_weight[...])
+        + dot_nt(dqkv[rows, cols : 2 * cols], key_weight[...])
+        + dot_nt(dqkv[rows, 2 * cols : 3 * cols], value_weight[...]),
+    )
+    first_sum.start()
+
+    g_output[...] = dot_tn(heads_own[...], residual_low[...]).astype(BF16)
+    sum_output.to_x()
+
+    def qkv_grads(i, _):
+        at = lanes(i * 256, 256)
+        g_qkv[span(i * 256, 256), :] = dot_tn(first_low[:, at], dqkv[...]).astype(BF16)
+        return 0
+
+    lax.fori_loop(0, width // 256, qkv_grads, 0)
+    sum_qkv.to_x()
+
+    sum_up.add_z()
+    sum_down.finish_z()
+    sum_output.add_x()
+
+    own_rows = span(own_start, half)
+    other_rows = span(sib_start, half)
+    i_out = links.take(2)
+    out_rows = mail.at[4]
+    token_rows = mail.at[8]
+
+    def finish_out(j, _):
+        out_sum.wait(j)
+
+        def body(s, _):
+            local = span(j * tile + s * SUB, SUB)
+            out_rows[local, :] = (
+                residual[local, :] + out_sum.rows(local) + row(down_bias)
+            ).astype(BF16)
+            return 0
+
+        lax.fori_loop(0, tile // SUB, body, 0)
+        return 0
+
+    def wait_far(j, _):
+        here = head_slot(j)
+        links.sent(out_sum.snd.at[here, :], out_sum.index + j)
+        links.sent(first_sum.snd.at[here, :], first_sum.index + j)
+        return 0
+
+    lax.fori_loop(0, half_tiles, wait_far, 0)
+    lax.fori_loop(0, half_tiles, finish_out, 0)
+    out_send = links.copy(out_rows, block_out.at[own_rows, :], i_out, sib)
+    out_send.start()
+    out_write = pltpu.make_async_copy(out_rows, block_out.at[own_rows, :], local_sems.at[0])
+    out_write.start()
+
+    sum_up.finish_z()
+    sum_down.back_x()
+    sum_output.add_z()
+    sum_qkv.add_x()
+
+    def first_back(j, _):
+        first_sum.wait(j)
+
+        def body(s, _):
+            local = span(j * tile + s * SUB, SUB)
+            rows = span(own_start + j * tile + s * SUB, SUB)
+            incoming = first_sum.rows(local)
+            v = tokens[rows, :].astype(F32)
+            e = v - jnp.mean(v, axis=-1, keepdims=True)
+            r = lax.rsqrt(jnp.mean(e * e, axis=-1, keepdims=True) + EPS)
+            xhat = e * r
+            token_rows[local, :] = (
+                residual_grad[local, :] + norm_back(incoming, xhat, r, row(first_gain))
+            ).astype(BF16)
+            add_to(0, incoming * xhat)
+            add_to(1, incoming)
+            return 0
+
+        lax.fori_loop(0, tile // SUB, body, 0)
+        return 0
+
+    lax.fori_loop(0, half_tiles, first_back, 0)
+    token_send = links.copy(token_rows, token_grad.at[own_rows, :], i_out + 1, sib)
+    token_send.start()
+    token_write = pltpu.make_async_copy(token_rows, token_grad.at[own_rows, :], local_sems.at[1])
+    token_write.start()
+
+    i_vec = links.take(1 + 2 * 7)
+    vec_send = links.copy(vec, vec_sib, i_vec, sib)
+    vec_send.start()
+
+    sum_qkv.add_z()
+    sum_output.finish_z()
+    sum_up.back_x()
+
+    links.got(vec_sib, i_vec)
+    vec_send.wait_send()
+    at_row = lax.broadcasted_iota(jnp.int32, vec.shape, 0)
+    vec[...] = vec[...] + jnp.where(at_row < 6, vec_sib[...], 0.0)
+    part = width // 8
+    vec_parts[dp] = vec[:, lanes(dp * part, part)]
+    part_sends = []
+    for k, peer in enumerate(dp_peers):
+        send = links.copy(
+            vec.at[:, lanes(peer[0] * part, part)], vec_parts.at[dp], i_vec + 1 + k, peer
+        )
+        send.start()
+        part_sends.append(send)
+
+    sum_qkv.finish_z()
+    sum_output.back_x()
+
+    for k in range(7):
+        links.got(vec_parts.at[(dp + 7 - k) % 8], i_vec + 1 + k)
+    total = vec_parts[0]
+    for k in range(1, 8):
+        total = total + vec_parts[k]
+    vec_sum[...] = total
+    vec_all[:, lanes(dp * part, part)] = total
+    for k, peer in enumerate(dp_peers):
+        send = links.copy(
+            vec_sum, vec_all.at[:, lanes(dp * part, part)], i_vec + 8 + k, peer
+        )
+        send.start()
+        part_sends.append(send)
+
+    sum_qkv.back_x()
+
+    writes = []
+    for n, each in enumerate((sum_down, sum_up, sum_output, sum_qkv)):
+        write = each.write(local_sems.at[2 + n])
+        write.start()
+        writes.append(write)
+
+    for k in range(7):
+        links.got(vec_all.at[:, lanes(((dp + 7 - k) % 8) * part, part)], i_vec + 8 + k)
+    vec_out[...] = vec_all[...]
+
+    for each in (sum_down, sum_up, sum_output, sum_qkv):
+        each.end()
+    for write in writes + [out_write, token_write]:
+        write.wait()
+    for send in wo_sends + part_sends + [out_send, token_send]:
+        send.wait_send()
+    links.got(block_out.at[other_rows, :], i_out)
+    links.got(token_grad.at[other_rows, :], i_out + 1)
+
+    def last_waits(j, _):
+        here = head_slot(j)
+        rows = span(own_start + j * tile, tile)
+        far_rows = span(sib_start + j * tile, tile)
+        links.sent(heads_own.at[rows, :], i_heads + j)
+        links.sent(heads_own.at[far_rows, :], i_heads + half_tiles + j)
+        links.sent(heads_own.at[far_rows, :], i_heads + 2 * half_tiles + j)
+        links.sent(second_low.at[rows, :], i_second + j)
+        links.sent(residual_low.at[rows, :], i_back + j)
+        links.sent(second_sum.snd.at[here, :], second_sum.index + j)
+        for each in (second_sum, out_sum, first_sum):
+            links.sent(each.cs.at[here, :], each.index + half_tiles + j)
+        return 0
+
+    lax.fori_loop(0, half_tiles, last_waits, 0)
+
+
+def kernel_shards(*args):
+    tokens, lengths = args[0], args[1]
+    n_rows, width = tokens.shape
+    count = n_rows // lengths.shape[0]
+    tile = 16 * count
+    half = n_rows // 2
+    cols = args[2].shape[1]
+    hidden = args[6].shape[1]
+    vmem = pltpu.VMEM
+    grads = ((hidden, width), (width, hidden), (cols, width), (width, 3 * cols))
+    halves = [(r // 2, n) for r, n in grads]
+    any_space = pl.BlockSpec(memory_space=pl.ANY)
+    in_vmem = pl.BlockSpec(memory_space=pltpu.VMEM)
+    scratch = [
+        vmem((n_rows, width), BF16),
+        vmem((n_rows, cols), BF16),
+        vmem((n_rows, cols), BF16),
+        vmem((n_rows, cols), BF16),
+        vmem((n_rows // tile * (cols // DH), tile, tile), F32),
+        vmem((n_rows, cols), BF16),
+        vmem((half, width), BF16),
+        vmem((width, width), BF16),
+        vmem((half, width), F32),
+        vmem((n_rows, width), BF16),
+        vmem((n_rows, hidden), BF16),
+        vmem((n_rows, hidden), BF16),
+        vmem((12, half, width), BF16),
+        vmem((half, width), F32),
+        vmem((n_rows, width), BF16),
+        vmem((n_rows, 3 * cols), BF16),
+    ]
+    scratch += [vmem(s, BF16) for s in grads]
+    for _ in range(4):
+        scratch += [vmem(s, BF16) for s in halves]
+    scratch += [
+        vmem((8, width), F32),
+        vmem((8, width), F32),
+        vmem((8, 8, width // 8), F32),
+        vmem((8, width // 8), F32),
+        vmem((8, width), F32),
+        pltpu.SemaphoreType.DMA((N_SEMS,)),
+        pltpu.SemaphoreType.DMA((N_SEMS,)),
+        pltpu.SemaphoreType.DMA((8,)),
+    ]
+    block_out, token_grad, down, up, output, qkv, vec = pl.pallas_call(
+        functools.partial(layer_kernel, count),
+        out_shape=[
+            jax.ShapeDtypeStruct((n_rows, width), BF16),
+            jax.ShapeDtypeStruct((n_rows, width), BF16),
+            *[jax.ShapeDtypeStruct(s, BF16) for s in grads],
+            jax.ShapeDtypeStruct((8, width), F32),
+        ],
+        in_specs=[in_vmem] * len(args),
+        out_specs=[any_space] * 6 + [in_vmem],
+        scratch_shapes=scratch,
+        compiler_params=pltpu.CompilerParams(
+            collective_id=0, has_side_effects=True, vmem_limit_bytes=63 * 2**20
+        ),
+        name="layer",
+    )(*args)
+    return (
+        block_out,
+        token_grad,
+        qkv[:, 0:cols].astype(F32),
+        qkv[:, cols : 2 * cols].astype(F32),
+        qkv[:, 2 * cols :].astype(F32),
+        output.astype(F32),
+        up.astype(F32),
+        vec[6, 0:hidden],
+        down.astype(F32),
+        vec[0],
+        vec[1],
+        vec[2],
+        vec[3],
+        vec[4],
+        vec[5],
+    )
+
+
 def solution(mesh):
+    fits = mesh.shape["dp"] == 8 and mesh.shape["tensor"] == 4
     return jax.shard_map(
-        shards,
+        kernel_shards if fits else plain_shards,
         mesh=mesh,
         in_specs=(
             P("dp", None),

time: 485 us -> 181 us (0.37)
  waiting for transfers between devices: 307 us -> 0 us
  Pallas kernels: 0 us -> 166 us
  blocking collectives: 63 us -> 0 us
  matrix products: 48.5 us -> 0 us
  other arithmetic: 33 us -> 7.43 us
  between operations: 14.5 us -> 0.68 us
  local copies, waits for them, and re-layouts: 16.9 us -> 5.26 us
    pallas_call x0 -> x1, Pallas kernels: none -> 166 us  [kernel_shards(): pl.pallas_call(functools.partial(layer_kernel, count), out_shape=[jax.Sha...]
    reduce_scatter x4 -> x0, waiting for transfers between devices: 128 us -> none  [the longest x1 43.2 us: shards(): lax.psum_scatter(attn_part, 'tensor', scatter_dimension=0, tiled=True)]
    psum x1 -> x0, waiting for transfers between devices: 121 us -> none  [shards(): lax.psum(query_grad.astype(jnp.bfloat16), 'dp').astype(jnp.float32)]
    psum x2 -> x0, blocking collectives: 63 us -> none  [the longest x1 41.7 us: shards(): lax.psum((first_gain_part, first_shift_part, second_gain_part, second_shi...]
    all_gather x4 -> x0, waiting for transfers between devices: 57.8 us -> none  [the longest x1 21.9 us: shards(): lax.all_gather(second_share.astype(jnp.bfloat16), 'tensor', axis=0, tiled...]
    dot_general x24 -> x0, matrix products: 48.5 us -> none  [the longest x1 6.69 us: shards(): jnp.einsum('td,fd->tf', cotangent, down_weight, preferred_element_type=jn...]
    convert_element_type x20 -> x4, other arithmetic: 19 us -> 7.43 us  [the longest x1 3.17 us: kernel_shards(): qkv[:, 2 * cols:].astype(F32)]
    reduce_sum x8 -> x0, other arithmetic: 11 us -> none  [the longest x2 3.71 us: norm_parts(): row_mean = jnp.mean(rows, axis=-1, keepdims=True)]
  transfers between devices with their start and end apart: 9 -> 0, of which waited for: 8 -> 0; matrix products, arithmetic and copies ran while one was open for 7% -> 0% of each run, Pallas kernels for 0% -> 0%
where the time goes in v1:
time: 181 us; the launch traced here: 179 us
  Pallas kernels  166 us (92%)
  other arithmetic  7.43 us (4%)
  local copies, waits for them, and re-layouts  5.26 us (3%)
    pallas_call x1, Pallas kernels, kernel_shards(): pl.pallas_call(functools.partial(layer_kernel, count), out_shape=[jax.Sha...  166 us
    unnamed x14, local copies, waits for them, and re-layouts  4.05 us

profile of v1, /device:TPU:0, one launch (start us, length us, event | category | flops | bytes accessed | tf_op | source)
XLA Modules:
  0.0 179.1 jit_solution(9635336877116451805)
XLA Ops:
  0.7 165.7 %layer.1 = (bf16[960,1024]{1,0:T(8,128)(2,1)}, bf16[960,1024]{1,0:T(8,128)(2,1)}, bf16[512,1024]{1,0:T(8,128)(2,1)}, bf16[1024,512]{1,0:T(8,128)(2,1)}, bf16[256...) custom-call(bf16[960,1024]{1,0:T(8,128)(2,1)} %tokens.1, s32[64]{0:T(128)} %lengths.1, ...), custom_call_target="tpu_custom_call" | custom-call | tf_op jit(solution)/shard_map/layer/pallas_call | solution.py:988
  166.4 0.0 copy-start.4
  166.4 3.2 %slice_convert_fusion = (f32[1024,256]{1,0:T(8,128)}, f32[1024,256]{1,0:T(8,128)}, f32[1024,256]{1,0:T(8,128)}) fusion(bf16[1024,768]{1,0:T(8,128)(2,1)} %get-tuple-element.24), kind=kLoop, calls=%fused_computation | loop fusion | flops 786432 | bytes 4718592 | tf_op jit(solution)/shard_map/convert_element_type | solution.py:1009
  169.6 0.0 copy-start.3
  169.6 0.0 copy-done.4
  169.6 1.1 convert_element_type.21
  170.7 0.0 copy-start.5
  170.7 0.0 copy-start.2
  170.7 0.5 copy-done.3
  171.2 1.6 convert_element_type.22
  172.8 0.0 copy-start.1
  172.8 0.0 copy-done.5
  172.8 0.6 slice.33
  173.4 0.0 copy-done.2
  173.4 1.6 convert_element_type.23
  175.0 0.6 fusion
  175.6 0.0 copy-done.1
  175.6 0.0 copy-start
  175.6 1.3 copy.33
  176.9 1.0 copy-done
  177.8 1.3 copy.34
Async XLA Ops:
  166.4 3.2 %copy-start.4 = (bf16[256,1024]{1,0:T(8,128)(2,1)S(1)}, bf16[256,1024]{1,0:T(8,128)(2,1)}, u32[]{:S(2)}) copy-start(bf16[256,1024]{1,0:T(8,128)(2,1)} %get-tuple-element.25) | copy-start | bytes 1572868
  169.6 1.6 copy-start.3
  170.7 2.1 %copy-start.5 = (f32[8,1024]{1,0:T(8,128)S(1)}, f32[8,1024]{1,0:T(8,128)}, u32[]{:S(2)}) copy-start(f32[8,1024]{1,0:T(8,128)} %get-tuple-element.27) | copy-start | bytes 98308
  170.7 2.7 %copy-start.2 = (bf16[512,1024]{1,0:T(8,128)(2,1)S(1)}, bf16[512,1024]{1,0:T(8,128)(2,1)}, u32[]{:S(2)}) copy-start(bf16[512,1024]{1,0:T(8,128)(2,1)} %get-tuple-element.28) | copy-start | bytes 3145732
  172.8 2.8 %copy-start.1 = (bf16[960,1024]{1,0:T(8,128)(2,1)S(1)}, bf16[960,1024]{1,0:T(8,128)(2,1)}, u32[]{:S(2)}) copy-start(bf16[960,1024]{1,0:T(8,128)(2,1)} %get-tuple-element.53) | copy-start | bytes 5898244
  175.6 2.3 %copy-start = (bf16[960,1024]{1,0:T(8,128)(2,1)S(1)}, bf16[960,1024]{1,0:T(8,128)(2,1)}, u32[]{:S(2)}) copy-start(bf16[960,1024]{1,0:T(8,128)(2,1)} %get-tuple-element.54) | copy-start | bytes 5898244

commit v2 on v1

--- a/solution.py
+++ b/solution.py
@@ -261,8 +261,27 @@
 F32 = jnp.float32
 BF16 = jnp.bfloat16
 MESH = pl.DeviceIdType.MESH
-SUB = 80
-N_SEMS = 128
+N_SEMS = 192
+
+PARTS = (
+    ("D", 0, 128, "a"), ("D", 128, 128, "d"), ("D", 256, 128, "d"), ("D", 384, 128, "a"),
+    ("U", 0, 256, "a"), ("U", 256, 256, "d"), ("U", 512, 256, "a"), ("U", 768, 256, "a"),
+    ("O", 0, 128, "a"), ("O", 128, 128, "a"), ("Q", 0, 128, "d"), ("Q", 128, 128, "d"),
+    ("Q", 256, 128, "a"), ("Q", 384, 128, "d"), ("Q", 512, 128, "a"), ("Q", 640, 128, "a"),
+    ("Q", 768, 128, "a"), ("Q", 896, 128, "d"),
+)
+ORDER = (
+    "U1", "S0", "D0", "S1", "D1", "V0", "T0", "U3", "T1", "U0", "5.1", "W0", "U2", "0.1", "V1",
+    "1.1", "3.1", "5.2", "2.1", "7.1", "1.2", "0.2", "4.1", "e5.3", "2.2", "B0", "3.2", "6.1",
+    "e1.3", "A0", "7.2", "0.3", "A1", "e2.3", "e5.4", "F0", "e1.4", "4.2", "3.3", "G0", "e0.4",
+    "e2.4", "6.2", "7.3", "B1", "e3.4", "5.5", "4.3", "A2", "A3", "e7.4", "6.3", "1.5", "Q1", "O0",
+    "e4.4", "Q3", "2.5", "5.6", "F1", "Q0", "Q2", "e6.4", "13.1", "1.6", "G1", "W1", "X0", "17.1",
+    "12.1", "2.6", "10.1", "8.1", "13.2", "11.1", "17.2", "9.1", "e13.3", "12.2", "10.2", "16.1",
+    "e17.3", "8.2", "Y0", "11.2", "14.1", "e10.3", "12.3", "9.2", "15.1", "e11.3", "e12.4",
+    "e13.4", "e8.4", "8.3", "16.2", "14.2", "9.3", "15.2", "16.3", "Y1", "Z0", "e17.4", "e9.4",
+    "14.3", "Z1", "e10.4", "e16.4", "e11.4", "e14.4", "13.5", "15.3", "17.5", "13.6", "Z2",
+    "e15.4", "10.5", "17.6", "X1", "11.5", "10.6", "11.6",
+)
 
 
 def dot(a, b):
@@ -315,22 +334,22 @@
 
 def layer_kernel(
     count,
-    tokens,
+    tokens_hbm,
     lengths,
-    query_weight,
-    key_weight,
-    value_weight,
-    output_weight,
-    up_weight,
+    query_hbm,
+    key_hbm,
+    value_hbm,
+    output_hbm,
+    up_hbm,
     up_bias,
-    down_weight,
+    down_hbm,
     first_gain,
     first_shift,
     second_gain,
     second_shift,
     output_bias,
     down_bias,
-    cotangent,
+    cotangent_hbm,
     block_out,
     token_grad,
     down_out,
@@ -338,6 +357,14 @@
     output_out,
     qkv_out,
     vec_out,
+    tokens,
+    cotangent,
+    query_weight,
+    key_weight,
+    value_weight,
+    wo_all,
+    up_weight,
+    down_weight,
     first_low,
     queries,
     key_rows,
@@ -345,7 +372,6 @@
     probs,
     heads_own,
     heads_full,
-    wo_all,
     residual,
     second_low,
     act,
@@ -406,9 +432,11 @@
     diag = (dp, t_diag)
     xp = (dp + 1 - 2 * x, t)
     adj = (dp + 2 - 4 * (z % 2), t)
+    cross = (dp + 2 - 4 * (z % 2) + 1 - 2 * x, t)
     mid = ((3 - z) * 2 + x, t)
     is_mid = jnp.logical_or(z == 1, z == 2)
     is_end = jnp.logical_or(z == 0, z == 3)
+    side = z // 2
     dp_peers = [((dp + k) % 8, t) for k in range(1, 8)]
     links = Links(sends, recvs, sib)
 
@@ -416,34 +444,95 @@
     for peer in [sib, opp, diag] + dp_peers:
         pl.semaphore_signal(barrier, inc=1, device_id=peer, device_id_type=MESH)
 
+    own_rows = span(c * half, half)
+    other_rows = span((1 - c) * half, half)
+    own_start = c * half
+    sib_start = (1 - c) * half
+    own_wo = span(t * cols, cols)
+
+    def turn_rows(i):
+        return span((i % 2) * half + (i // 2) * tile, tile)
+
+    def token_load(i):
+        rows = turn_rows(i)
+        return pltpu.make_async_copy(tokens_hbm.at[rows, :], tokens.at[rows, :], local_sems.at[i])
+
+    loads = [
+        pltpu.make_async_copy(src, dst, local_sems.at[n_tiles + n])
+        for n, (src, dst) in enumerate(
+            (
+                (query_hbm, query_weight),
+                (key_hbm, key_weight),
+                (value_hbm, value_weight),
+                (output_hbm, wo_all.at[own_wo, :]),
+                (up_hbm, up_weight),
+                (down_hbm, down_weight),
+                (cotangent_hbm, cotangent),
+            )
+        )
+    ]
+    token_load(0).start()
+    for load in loads[:3]:
+        load.start()
+    for i in range(1, n_tiles):
+        token_load(i).start()
+    for load in loads[3:]:
+        load.start()
+    free_sem = n_tiles + len(loads)
+
     def row(ref):
         return ref[...].astype(F32).reshape(1, ref.shape[0])
 
-    own_start = c * half
-    sib_start = (1 - c) * half
-
-    def first_norm(i, _):
-        rows = span(i * SUB, SUB)
-        v = tokens[rows, :].astype(F32)
+    def norm_parts(v):
         e = v - jnp.mean(v, axis=-1, keepdims=True)
         r = lax.rsqrt(jnp.mean(e * e, axis=-1, keepdims=True) + EPS)
-        first_low[rows, :] = (e * r * row(first_gain) + row(first_shift)).astype(BF16)
-        return 0
-
-    lax.fori_loop(0, n_rows // SUB, first_norm, 0)
-
-    pl.semaphore_wait(barrier, 10)
-
-    wo_rows = [span(v * cols, cols) for v in (t, t_sib, t_opp, t_diag)]
-    wo_all[wo_rows[0], :] = output_weight[...]
-    i_wo = links.take(3)
-    wo_sends = [
-        links.copy(output_weight, wo_all.at[wo_rows[0], :], i_wo, opp),
-        links.copy(output_weight, wo_all.at[wo_rows[0], :], i_wo + 1, sib),
-        links.copy(wo_all.at[wo_rows[2], :], wo_all.at[wo_rows[2], :], i_wo + 2, sib),
+        return e * r, r
+
+    piece = cols // 4
+    quarter = x + 2 * (z % 2)
+
+    def wo_piece(owner, number):
+        return wo_all.at[span(owner * cols + number * piece, piece), :]
+
+    i_wo = links.take(9)
+    by_y = links.copy(
+        output_hbm.at[span(quarter * piece, piece), :], wo_piece(t, quarter), i_wo, opp
+    )
+    whole_to_sib = links.copy(output_hbm, wo_all.at[own_wo, :], i_wo + 1, sib)
+    q_xp, q_adj = quarter + 1 - 2 * x, quarter + 2 - 4 * (z % 2)
+    q_cross = q_adj + 1 - 2 * x
+    mine = wo_piece(t_opp, quarter)
+    to_x = links.copy(mine, mine, i_wo + 2, xp)
+    to_z = links.copy(mine, mine, i_wo + 3, adj)
+    from_x = wo_piece(t_opp, q_xp)
+    on_z = links.copy(from_x, from_x, i_wo + 4, adj)
+    others = ((quarter, None), (q_xp, i_wo + 2), (q_adj, i_wo + 3), (q_cross, i_wo + 4))
+    relays = [
+        links.copy(wo_piece(t_opp, q), wo_piece(t_opp, q), i_wo + 5 + n, sib)
+        for n, (q, _i) in enumerate(others)
     ]
-    wo_sends[0].start()
-    wo_sends[1].start()
+
+    def share_first():
+        links.got(mine, i_wo)
+        to_x.start()
+        to_z.start()
+        relays[0].start()
+
+    def share_next():
+        links.got(from_x, i_wo + 2)
+        on_z.start()
+        relays[1].start()
+
+    def share_last():
+        links.got(wo_piece(t_opp, q_adj), i_wo + 3)
+        relays[2].start()
+        links.got(wo_piece(t_opp, q_cross), i_wo + 4)
+        relays[3].start()
+        links.got(wo_all.at[span(t_sib * cols, cols), :], i_wo + 1)
+        for n, q in enumerate((quarter, q_xp, q_adj, q_cross)):
+            links.got(wo_piece(t_diag, q), i_wo + 5 + n)
+
+    wo_sends = [by_y, whole_to_sib, to_x, to_z, on_z] + relays
 
     def allowed_of(number):
         def series_of(index):
@@ -472,7 +561,16 @@
     def attend(i, _):
         h, j = i % 2, i // 2
         number = h * half_tiles + j
-        rows = span(number * tile, tile)
+        rows = turn_rows(i)
+        token_load(i).wait()
+        xhat, _r = norm_parts(tokens[rows, :].astype(F32))
+        first_low[rows, :] = (xhat * row(first_gain) + row(first_shift)).astype(BF16)
+
+        @pl.when(i == 0)
+        def _():
+            for load in loads[:3]:
+                load.wait()
+
         normed = first_low[rows, :]
         q = dot(normed, query_weight[...]).astype(BF16)
         k = dot(normed, key_weight[...]).astype(BF16)
@@ -480,6 +578,13 @@
         queries[rows, :] = q
         key_rows[rows, :] = k
         value_rows[rows, :] = v
+
+        @pl.when(i == 0)
+        def _():
+            pl.semaphore_wait(barrier, 10)
+            by_y.start()
+            whole_to_sib.start()
+
         allowed = allowed_of(number)
         for head in range(heads_here):
             at = slice(head * DH, (head + 1) * DH)
@@ -500,58 +605,27 @@
             links.copy(heads_own.at[rows, :], slot, i_heads + half_tiles + j, sib).start()
             links.copy(heads_own.at[rows, :], slot, i_heads + 2 * half_tiles + j, diag).start()
 
+        @pl.when(i == 3)
+        def _():
+            share_first()
+
         return 0
 
     lax.fori_loop(0, n_tiles, attend, 0)
 
-    links.got(wo_all.at[wo_rows[2], :], i_wo)
-    wo_sends[2].start()
-    links.got(wo_all.at[wo_rows[1], :], i_wo + 1)
-    links.got(wo_all.at[wo_rows[3], :], i_wo + 2)
+    share_next()
+    for load in loads[3:]:
+        load.wait()
+    share_last()
 
     i_second = links.take(half_tiles)
-
-    def residual_stats(rows):
-        v = residual[rows, :]
-        e = v - jnp.mean(v, axis=-1, keepdims=True)
-        r = lax.rsqrt(jnp.mean(e * e, axis=-1, keepdims=True) + EPS)
-        return e * r, r
-
-    def project(j, _):
-        here = head_slot(j)
-        for n, who in enumerate((t_opp, t_sib, t_diag)):
-            links.got(heads_full.at[here, lanes(who * cols, cols)], i_heads + n * half_tiles + j)
-        rows = span(own_start + j * tile, tile)
-        residual[here, :] = (
-            tokens[rows, :].astype(F32) + dot(heads_full[here, :], wo_all[...]) + row(output_bias)
-        )
-
-        def second_norm(s, _):
-            local = span(j * tile + s * SUB, SUB)
-            xhat, _r = residual_stats(local)
-            second_low[span(own_start + j * tile + s * SUB, SUB), :] = (
-                xhat * row(second_gain) + row(second_shift)
-            ).astype(BF16)
-            return 0
-
-        lax.fori_loop(0, tile // SUB, second_norm, 0)
-        links.copy(second_low.at[rows, :], second_low.at[rows, :], i_second + j, sib).start()
-        return 0
-
-    lax.fori_loop(0, half_tiles, project, 0)
-
     vec[...] = jnp.zeros_like(vec)
 
     def in_turn(i):
         return jnp.where(i % 2 == 0, own_start, sib_start) + (i // 2) * tile
 
-    def feed(i, _):
+    def feed(i):
         rows = span(in_turn(i), tile)
-
-        @pl.when(i % 2 == 1)
-        def _():
-            links.got(second_low.at[rows, :], i_second + i // 2)
-
         u = dot(second_low[rows, :], up_weight[...]) + row(up_bias)
         big = 0.5 * (1.0 + lax.erf(u * (1.0 / math.sqrt(2.0))))
         act[rows, :] = (u * big).astype(BF16)
@@ -559,95 +633,214 @@
         grad = (dot_nt(cotangent[rows, :], down_weight[...]) * slope).astype(BF16)
         ugp[rows, :] = grad
         vec[6:7, 0:hidden] += jnp.sum(grad.astype(F32), axis=0, keepdims=True)
+
+    def project(j, _):
+        here = head_slot(j)
+        for n, who in enumerate((t_opp, t_sib, t_diag)):
+            links.got(heads_full.at[here, lanes(who * cols, cols)], i_heads + n * half_tiles + j)
+        rows = span(own_start + j * tile, tile)
+        v = tokens[rows, :].astype(F32) + dot(heads_full[here, :], wo_all[...]) + row(output_bias)
+        residual[here, :] = v
+        xhat, _r = norm_parts(v)
+        second_low[rows, :] = (xhat * row(second_gain) + row(second_shift)).astype(BF16)
+        links.copy(second_low.at[rows, :], second_low.at[rows, :], i_second + j, sib).start()
+        feed(2 * j)
+        links.got(second_low.at[span(sib_start + j * tile, tile), :], i_second + j)
+        feed(2 * j + 1)
         return 0
 
-    lax.fori_loop(0, n_tiles, feed, 0)
-
-    class Sum:
+    lax.fori_loop(0, half_tiles, project, 0)
+
+    class Tensor:
         def __init__(self, grads, rx, rz, rm, total, out):
             self.grads, self.rx, self.rz, self.rm, self.total, self.out = (
                 grads, rx, rz, rm, total, out,
             )
-            self.size = grads.shape[0] // 2
-            self.mine = span(x * self.size, self.size)
-            self.other = span((1 - x) * self.size, self.size)
-            self.index = links.take(5)
-
-        def add(self, into, take):
-            step = 32
-
-            def body(i, _):
-                at = span(i * step, step)
-                own = span(x * self.size + i * step, step)
-                into[at if into is self.total else own, :] = (
-                    self.grads[own, :].astype(F32) + take[at, :].astype(F32)
-                ).astype(BF16)
-                return 0
-
-            lax.fori_loop(0, self.size // step, body, 0)
-
-        def to_x(self):
-            links.copy(self.grads.at[self.other, :], self.rx, self.index, xp).start()
-
-        def add_x(self):
-            links.got(self.rx, self.index)
-            self.add(self.grads, self.rx)
+
+    tensors = {
+        "D": Tensor(g_down, rx_down, rz_down, rm_down, t_down, down_out),
+        "U": Tensor(g_up, rx_up, rz_up, rm_up, t_up, up_out),
+        "O": Tensor(g_output, rx_output, rz_output, rm_output, t_output, output_out),
+        "Q": Tensor(g_qkv, rx_qkv, rz_qkv, rm_qkv, t_qkv, qkv_out),
+    }
+
+    class Part:
+        def __init__(self, tensor, start, size, sem):
+            self.size = size // 2
+            self.start = start
+            here = pl.ds(start // 2, self.size)
+            self.grads, self.out = tensor.grads, tensor.out
+            self.rx, self.rz, self.rm, self.total = (
+                ref.at[here, :] for ref in (tensor.rx, tensor.rz, tensor.rm, tensor.total)
+            )
+            self.index = links.take(self.messages)
+            self.sem = sem
+
+        def half_at(self, which):
+            return span(self.start + which * self.size, self.size)
+
+        def send(self, src, dst, message, device):
+            links.copy(src, dst, self.index + message, device).start()
+
+        def got(self, dst, message):
+            links.got(dst, self.index + message)
+
+        def sent(self, src, message):
+            links.sent(src, self.index + message)
+
+        def add(self, rows, came):
+            return (self.grads[rows, :].astype(F32) + came[...].astype(F32)).astype(BF16)
+
+        def write(self, rows):
+            return pltpu.make_async_copy(self.total, self.out.at[rows, :], local_sems.at[self.sem])
+
+    class PartX(Part):
+        messages = 5
+
+        def begin(self):
+            self.send(self.grads.at[self.half_at(1 - x), :], self.rx, 0, xp)
+
+        def step(self, number):
+            mine = self.half_at(x)
+            grads, out = self.grads.at[mine, :], self.out.at[mine, :]
+            if number == 1:
+                self.got(self.rx, 0)
+                self.grads[mine, :] = self.add(mine, self.rx)
+
+                @pl.when(is_end)
+                def _():
+                    self.send(grads, self.rz, 1, adj)
+
+            if number == 2:
+
+                @pl.when(is_mid)
+                def _():
+                    self.got(self.rz, 1)
+                    self.grads[mine, :] = self.add(mine, self.rz)
+                    self.send(grads, self.rm, 2, mid)
+
+            if number == 3:
+
+                @pl.when(is_mid)
+                def _():
+                    self.got(self.rm, 2)
+                    self.total[...] = self.add(mine, self.rm)
+                    self.send(self.total, out, 3, adj)
+                    self.send(self.total, out, 4, xp)
+                    self.write(mine).start()
+
+            if number == 4:
+
+                @pl.when(is_end)
+                def _():
+                    self.got(out, 3)
+                    self.send(out, out, 4, xp)
+
+        def end(self):
+            mine, other = self.half_at(x), self.half_at(1 - x)
+            grads, out = self.grads.at[mine, :], self.out.at[mine, :]
+            self.sent(self.grads.at[other, :], 0)
+            self.got(self.out.at[other, :], 4)
 
             @pl.when(is_end)
             def _():
-                links.copy(self.grads.at[self.mine, :], self.rz, self.index + 1, adj).start()
-
-        def add_z(self):
+                self.sent(grads, 1)
+                self.sent(out, 4)
+
             @pl.when(is_mid)
             def _():
-                links.got(self.rz, self.index + 1)
-                self.add(self.grads, self.rz)
-                links.copy(self.grads.at[self.mine, :], self.rm, self.index + 2, mid).start()
-
-        def finish_z(self):
+                self.sent(grads, 2)
+                self.sent(self.total, 3)
+                self.sent(self.total, 4)
+                self.write(mine).wait()
+
+    class PartZ(Part):
+        messages = 7
+
+        def begin(self):
+            far = self.grads.at[self.half_at(1 - side), :]
+
+            @pl.when(is_end)
+            def _():
+                self.send(far, self.rz, 0, adj)
+
+        def step(self, number):
+            near, far = self.half_at(side), self.half_at(1 - side)
+
+            @pl.when(is_end if number in (3, 4) else is_mid)
+            def _():
+                if number == 1:
+                    self.got(self.rz, 0)
+                    self.grads[far, :] = self.add(far, self.rz)
+                    self.send(self.grads.at[far, :], self.rm, 1, mid)
+                if number == 2:
+                    self.got(self.rm, 1)
+                    self.grads[near, :] = self.add(near, self.rm)
+                    self.send(self.grads.at[near, :], self.rz, 2, adj)
+                if number == 3:
+                    self.got(self.rz, 2)
+                    self.grads[near, :] = self.add(near, self.rz)
+                    self.send(self.grads.at[near, :], self.rx, 3, xp)
+                if number == 4:
+                    self.got(self.rx, 3)
+                    self.total[...] = self.add(near, self.rx)
+                    self.send(self.total, self.out.at[near, :], 4, adj)
+                    self.write(near).start()
+                if number == 5:
+                    self.got(self.out.at[near, :], 4)
+                    self.send(self.out.at[near, :], self.out.at[near, :], 5, mid)
+                if number == 6:
+                    self.got(self.out.at[far, :], 5)
+                    self.send(self.out.at[far, :], self.out.at[far, :], 6, adj)
+
+        def end(self):
+            near, far = self.half_at(side), self.half_at(1 - side)
+
+            @pl.when(is_end)
+            def _():
+                self.got(self.out.at[far, :], 6)
+                self.sent(self.grads.at[far, :], 0)
+                self.sent(self.grads.at[near, :], 3)
+                self.sent(self.total, 4)
+                self.write(near).wait()
+
             @pl.when(is_mid)
             def _():
-                links.got(self.rm, self.index + 2)
-                self.add(self.total, self.rm)
-                links.copy(self.total, self.total, self.index + 3, adj).start()
-                links.copy(self.total, self.out.at[self.mine, :], self.index + 4, xp).start()
-
-        def back_x(self):
-            @pl.when(is_end)
-            def _():
-                links.got(self.total, self.index + 3)
-                links.copy(self.total, self.out.at[self.mine, :], self.index + 4, xp).start()
-
-        def write(self, sem):
-            return pltpu.make_async_copy(self.total, self.out.at[self.mine, :], sem)
-
-        def end(self):
-            links.got(self.out.at[self.other, :], self.index + 4)
-            links.sent(self.grads.at[self.other, :], self.index)
-
-            @pl.when(is_end)
-            def _():
-                links.sent(self.grads.at[self.mine, :], self.index + 1)
-
-            @pl.when(is_mid)
-            def _():
-                links.sent(self.grads.at[self.mine, :], self.index + 2)
-                links.sent(self.total, self.index + 3)
-
-            links.sent(self.total, self.index + 4)
-
-    sum_down = Sum(g_down, rx_down, rz_down, rm_down, t_down, down_out)
-    sum_up = Sum(g_up, rx_up, rz_up, rm_up, t_up, up_out)
-    sum_output = Sum(g_output, rx_output, rz_output, rm_output, t_output, output_out)
-    sum_qkv = Sum(g_qkv, rx_qkv, rz_qkv, rm_qkv, t_qkv, qkv_out)
-
-    def down_grads(i, _):
-        at = lanes(i * 256, 256)
-        g_down[span(i * 256, 256), :] = dot_tn(act[:, at], cotangent[...]).astype(BF16)
-        return 0
-
-    lax.fori_loop(0, hidden // 256, down_grads, 0)
-    sum_down.to_x()
+                self.sent(self.grads.at[far, :], 1)
+                self.sent(self.grads.at[near, :], 2)
+                self.sent(self.out.at[near, :], 5)
+                self.sent(self.out.at[far, :], 6)
+
+    parts = [
+        {"a": PartX, "d": PartZ}[kind](tensors[name], start, size, free_sem + n)
+        for n, (name, start, size, kind) in enumerate(PARTS)
+    ]
+
+    def begin_parts(name, first, size):
+        for (which, start, rows, _kind), part in zip(PARTS, parts, strict=True):
+            if which == name and first < start + rows <= first + size:
+                part.begin()
+
+    block = 256
+
+    def down_grads(i):
+        at = slice(i * block, (i + 1) * block)
+        g_down[at, :] = dot_tn(act[:, at], cotangent[...]).astype(BF16)
+        begin_parts("D", i * block, block)
+
+    def up_grads(i):
+        at = slice(i * block, (i + 1) * block)
+        g_up[at, :] = dot_tn(second_low[:, at], ugp[...]).astype(BF16)
+        begin_parts("U", i * block, block)
+
+    def output_grads(_i):
+        g_output[...] = dot_tn(heads_own[...], residual_low[...]).astype(BF16)
+        begin_parts("O", 0, cols)
+
+    def qkv_grads(i):
+        at = slice(i * block, (i + 1) * block)
+        g_qkv[at, :] = dot_tn(first_low[:, at], dqkv[...]).astype(BF16)
+        begin_parts("Q", i * block, block)
 
     class RowSum:
         def __init__(self, number, part):
@@ -655,54 +848,39 @@
             self.part = part
             self.index = links.take(2 * half_tiles)
 
-        def start(self):
-            def far(j, _):
-                here = head_slot(j)
-                self.snd[here, :] = self.part(span(sib_start + j * tile, tile)).astype(BF16)
-                links.copy(self.snd.at[here, :], self.r1.at[here, :], self.index + j, sib).start()
-                return 0
-
-            def near(j, _):
-                here = head_slot(j)
-                mine = self.part(span(own_start + j * tile, tile))
-                links.got(self.r1.at[here, :], self.index + j)
-                self.cs[here, :] = (mine + self.r1[here, :].astype(F32)).astype(BF16)
-                links.copy(
-                    self.cs.at[here, :], self.r2.at[here, :], self.index + half_tiles + j, opp
-                ).start()
-                return 0
-
-            lax.fori_loop(0, half_tiles, far, 0)
-            lax.fori_loop(0, half_tiles, near, 0)
-
-        def wait(self, j):
-            links.got(self.r2.at[head_slot(j), :], self.index + half_tiles + j)
-
-        def rows(self, local):
-            return self.cs[local, :].astype(F32) + self.r2[local, :].astype(F32)
-
-        def end(self):
-            def body(j, _):
-                here = head_slot(j)
-                links.sent(self.snd.at[here, :], self.index + j)
-                links.sent(self.cs.at[here, :], self.index + half_tiles + j)
-                return 0
-
-            lax.fori_loop(0, half_tiles, body, 0)
+        def far(self, j):
+            here = head_slot(j)
+            self.snd[here, :] = self.part(span(sib_start + j * tile, tile)).astype(BF16)
+            links.copy(self.snd.at[here, :], self.r1.at[here, :], self.index + j, sib).start()
+
+        def near(self, j):
+            here = head_slot(j)
+            mine = self.part(span(own_start + j * tile, tile))
+            links.got(self.r1.at[here, :], self.index + j)
+            self.cs[here, :] = (mine + self.r1[here, :].astype(F32)).astype(BF16)
+            links.copy(
+                self.cs.at[here, :], self.r2.at[here, :], self.index + half_tiles + j, opp
+            ).start()
+
+        def rows(self, j):
+            here = head_slot(j)
+            links.got(self.r2.at[here, :], self.index + half_tiles + j)
+            return self.cs[here, :].astype(F32) + self.r2[here, :].astype(F32)
+
+        def end(self, j):
+            here = head_slot(j)
+            links.sent(self.snd.at[here, :], self.index + j)
+            links.sent(self.cs.at[here, :], self.index + half_tiles + j)
 
     second_sum = RowSum(0, lambda rows: dot_nt(ugp[rows, :], up_weight[...]))
-    second_sum.start()
-
-    def up_grads(i, _):
-        at = lanes(i * 256, 256)
-        g_up[span(i * 256, 256), :] = dot_tn(second_low[:, at], ugp[...]).astype(BF16)
-        return 0
-
-    lax.fori_loop(0, width // 256, up_grads, 0)
-    sum_up.to_x()
-
     out_sum = RowSum(1, lambda rows: dot(act[rows, :], down_weight[...]))
-    out_sum.start()
+    first_sum = RowSum(
+        2,
+        lambda rows: dot_nt(dqkv[rows, 0:cols], query_weight[...])
+        + dot_nt(dqkv[rows, cols : 2 * cols], key_weight[...])
+        + dot_nt(dqkv[rows, 2 * cols : 3 * cols], value_weight[...]),
+    )
+    row_sums = (second_sum, out_sum, first_sum)
 
     i_back = links.take(half_tiles)
 
@@ -717,44 +895,28 @@
             - xhat * jnp.mean(weighted * xhat, axis=-1, keepdims=True)
         )
 
-    def second_back(j, _):
-        second_sum.wait(j)
-
-        def body(s, _):
-            local = span(j * tile + s * SUB, SUB)
-            rows = span(own_start + j * tile + s * SUB, SUB)
-            incoming = second_sum.rows(local)
-            xhat, r = residual_stats(local)
-            given = cotangent[rows, :].astype(F32)
-            grad = given + norm_back(incoming, xhat, r, row(second_gain))
-            residual_grad[local, :] = grad
-            residual_low[rows, :] = grad.astype(BF16)
-            add_to(2, incoming * xhat)
-            add_to(3, incoming)
-            add_to(4, grad)
-            add_to(5, given)
-            return 0
-
-        lax.fori_loop(0, tile // SUB, body, 0)
+    def second_back(j):
+        local = head_slot(j)
         rows = span(own_start + j * tile, tile)
+        incoming = second_sum.rows(j)
+        xhat, r = norm_parts(residual[local, :])
+        given = cotangent[rows, :].astype(F32)
+        grad = given + norm_back(incoming, xhat, r, row(second_gain))
+        residual_grad[local, :] = grad
+        residual_low[rows, :] = grad.astype(BF16)
         links.copy(residual_low.at[rows, :], residual_low.at[rows, :], i_back + j, sib).start()
-        return 0
-
-    lax.fori_loop(0, half_tiles, second_back, 0)
-
-    sum_down.add_x()
-    sum_up.add_x()
-
-    def attend_back(i, _):
+        add_to(2, incoming * xhat)
+        add_to(3, incoming)
+        add_to(4, grad)
+        add_to(5, given)
+
+    def attend_back(i):
         start = in_turn(i)
         rows = span(start, tile)
         number = start // tile
-
-        @pl.when(i % 2 == 1)
-        def _():
+        if i % 2 == 1:
             links.got(residual_low.at[rows, :], i_back + i // 2)
-
-        grads = dot_nt(residual_low[rows, :], output_weight[...]).astype(BF16)
+        grads = dot_nt(residual_low[rows, :], wo_all[own_wo, :]).astype(BF16)
         for head in range(heads_here):
             at = slice(head * DH, (head + 1) * DH)
             share = probs[number * heads_here + head]
@@ -771,174 +933,150 @@
             dqkv[rows, 2 * cols + head * DH : 2 * cols + (head + 1) * DH] = dot_tn(
                 share.astype(BF16), grads[:, at]
             ).astype(BF16)
-        return 0
-
-    lax.fori_loop(0, n_tiles, attend_back, 0)
-
-    sum_down.add_z()
-
-    first_sum = RowSum(
-        2,
-        lambda rows: dot_nt(dqkv[rows, 0:cols], query_weight[...])
-        + dot_nt(dqkv[rows, cols : 2 * cols], key_weight[...])
-        + dot_nt(dqkv[rows, 2 * cols : 3 * cols], value_weight[...]),
-    )
-    first_sum.start()
-
-    g_output[...] = dot_tn(heads_own[...], residual_low[...]).astype(BF16)
-    sum_output.to_x()
-
-    def qkv_grads(i, _):
-        at = lanes(i * 256, 256)
-        g_qkv[span(i * 256, 256), :] = dot_tn(first_low[:, at], dqkv[...]).astype(BF16)
-        return 0
-
-    lax.fori_loop(0, width // 256, qkv_grads, 0)
-    sum_qkv.to_x()
-
-    sum_up.add_z()
-    sum_down.finish_z()
-    sum_output.add_x()
-
-    own_rows = span(own_start, half)
-    other_rows = span(sib_start, half)
-    i_out = links.take(2)
+
+    i_out = links.take(2 * half_tiles)
     out_rows = mail.at[4]
     token_rows = mail.at[8]
-
-    def finish_out(j, _):
-        out_sum.wait(j)
-
-        def body(s, _):
-            local = span(j * tile + s * SUB, SUB)
-            out_rows[local, :] = (
-                residual[local, :] + out_sum.rows(local) + row(down_bias)
-            ).astype(BF16)
-            return 0
-
-        lax.fori_loop(0, tile // SUB, body, 0)
-        return 0
-
-    def wait_far(j, _):
-        here = head_slot(j)
-        links.sent(out_sum.snd.at[here, :], out_sum.index + j)
-        links.sent(first_sum.snd.at[here, :], first_sum.index + j)
-        return 0
-
-    lax.fori_loop(0, half_tiles, wait_far, 0)
-    lax.fori_loop(0, half_tiles, finish_out, 0)
-    out_send = links.copy(out_rows, block_out.at[own_rows, :], i_out, sib)
-    out_send.start()
-    out_write = pltpu.make_async_copy(out_rows, block_out.at[own_rows, :], local_sems.at[0])
-    out_write.start()
-
-    sum_up.finish_z()
-    sum_down.back_x()
-    sum_output.add_z()
-    sum_qkv.add_x()
-
-    def first_back(j, _):
-        first_sum.wait(j)
-
-        def body(s, _):
-            local = span(j * tile + s * SUB, SUB)
-            rows = span(own_start + j * tile + s * SUB, SUB)
-            incoming = first_sum.rows(local)
-            v = tokens[rows, :].astype(F32)
-            e = v - jnp.mean(v, axis=-1, keepdims=True)
-            r = lax.rsqrt(jnp.mean(e * e, axis=-1, keepdims=True) + EPS)
-            xhat = e * r
-            token_rows[local, :] = (
-                residual_grad[local, :] + norm_back(incoming, xhat, r, row(first_gain))
-            ).astype(BF16)
-            add_to(0, incoming * xhat)
-            add_to(1, incoming)
-            return 0
-
-        lax.fori_loop(0, tile // SUB, body, 0)
-        return 0
-
-    lax.fori_loop(0, half_tiles, first_back, 0)
-    token_send = links.copy(token_rows, token_grad.at[own_rows, :], i_out + 1, sib)
-    token_send.start()
-    token_write = pltpu.make_async_copy(token_rows, token_grad.at[own_rows, :], local_sems.at[1])
-    token_write.start()
+    out_sem = free_sem + len(PARTS)
+
+    def finished(j, number, rows_ref, out):
+        rows = span(own_start + j * tile, tile)
+        src = rows_ref.at[head_slot(j), :]
+        n = number * half_tiles + j
+        return (
+            links.copy(src, out.at[rows, :], i_out + n, sib),
+            pltpu.make_async_copy(src, out.at[rows, :], local_sems.at[out_sem + n]),
+        )
+
+    def finish_out(j):
+        local = head_slot(j)
+        links.sent(out_sum.snd.at[local, :], out_sum.index + j)
+        out_rows[local, :] = (residual[local, :] + out_sum.rows(j) + row(down_bias)).astype(BF16)
+        for each in finished(j, 0, out_rows, block_out):
+            each.start()
+
+    def first_back(j):
+        local = head_slot(j)
+        rows = span(own_start + j * tile, tile)
+        incoming = first_sum.rows(j)
+        xhat, r = norm_parts(tokens[rows, :].astype(F32))
+        grad = residual_grad[local, :] + norm_back(incoming, xhat, r, row(first_gain))
+        links.sent(first_sum.snd.at[local, :], first_sum.index + j)
+        token_rows[local, :] = grad.astype(BF16)
+        for each in finished(j, 1, token_rows, token_grad):
+            each.start()
+        add_to(0, incoming * xhat)
+        add_to(1, incoming)
 
     i_vec = links.take(1 + 2 * 7)
     vec_send = links.copy(vec, vec_sib, i_vec, sib)
-    vec_send.start()
-
-    sum_qkv.add_z()
-    sum_output.finish_z()
-    sum_up.back_x()
-
-    links.got(vec_sib, i_vec)
-    vec_send.wait_send()
-    at_row = lax.broadcasted_iota(jnp.int32, vec.shape, 0)
-    vec[...] = vec[...] + jnp.where(at_row < 6, vec_sib[...], 0.0)
     part = width // 8
-    vec_parts[dp] = vec[:, lanes(dp * part, part)]
-    part_sends = []
-    for k, peer in enumerate(dp_peers):
-        send = links.copy(
-            vec.at[:, lanes(peer[0] * part, part)], vec_parts.at[dp], i_vec + 1 + k, peer
-        )
-        send.start()
-        part_sends.append(send)
-
-    sum_qkv.finish_z()
-    sum_output.back_x()
-
-    for k in range(7):
-        links.got(vec_parts.at[(dp + 7 - k) % 8], i_vec + 1 + k)
-    total = vec_parts[0]
-    for k in range(1, 8):
-        total = total + vec_parts[k]
-    vec_sum[...] = total
-    vec_all[:, lanes(dp * part, part)] = total
-    for k, peer in enumerate(dp_peers):
-        send = links.copy(
-            vec_sum, vec_all.at[:, lanes(dp * part, part)], i_vec + 8 + k, peer
-        )
-        send.start()
-        part_sends.append(send)
-
-    sum_qkv.back_x()
-
-    writes = []
-    for n, each in enumerate((sum_down, sum_up, sum_output, sum_qkv)):
-        write = each.write(local_sems.at[2 + n])
-        write.start()
-        writes.append(write)
+    mine_at = lanes(dp * part, part)
+    part_sends = [
+        links.copy(vec.at[:, lanes(peer[0] * part, part)], vec_parts.at[dp], i_vec + 1 + k, peer)
+        for k, peer in enumerate(dp_peers)
+    ]
+    sum_sends = [
+        links.copy(vec_sum, vec_all.at[:, mine_at], i_vec + 8 + k, peer)
+        for k, peer in enumerate(dp_peers)
+    ]
+
+    def vectors(number):
+        if number == 0:
+            vec_send.start()
+        if number == 1:
+            links.got(vec_sib, i_vec)
+            vec_send.wait_send()
+            at_row = lax.broadcasted_iota(jnp.int32, vec.shape, 0)
+            vec[...] = vec[...] + jnp.where(at_row < 6, vec_sib[...], 0.0)
+            vec_parts[dp] = vec[:, mine_at]
+            for send in part_sends:
+                send.start()
+        if number == 2:
+            for k in range(7):
+                links.got(vec_parts.at[(dp + 7 - k) % 8], i_vec + 1 + k)
+            total = vec_parts[0]
+            for k in range(1, 8):
+                total = total + vec_parts[k]
+            vec_sum[...] = total
+            vec_all[:, mine_at] = total
+            for send in sum_sends:
+                send.start()
+
+    tasks = {
+        "D": down_grads,
+        "U": up_grads,
+        "O": output_grads,
+        "Q": qkv_grads,
+        "S": second_sum.far,
+        "T": second_sum.near,
+        "V": out_sum.far,
+        "W": out_sum.near,
+        "F": first_sum.far,
+        "G": first_sum.near,
+        "B": second_back,
+        "A": attend_back,
+        "X": finish_out,
+        "Y": first_back,
+        "Z": vectors,
+    }
+    for name in ORDER:
+        if "." in name:
+            number, step = name.removeprefix("e").split(".")
+            parts[int(number)].step(int(step))
+        else:
+            tasks[name[0]](int(name[1:]))
 
     for k in range(7):
         links.got(vec_all.at[:, lanes(((dp + 7 - k) % 8) * part, part)], i_vec + 8 + k)
     vec_out[...] = vec_all[...]
-
-    for each in (sum_down, sum_up, sum_output, sum_qkv):
+    for each in parts:
         each.end()
-    for write in writes + [out_write, token_write]:
-        write.wait()
-    for send in wo_sends + part_sends + [out_send, token_send]:
+    for send in wo_sends + part_sends + sum_sends:
         send.wait_send()
-    links.got(block_out.at[other_rows, :], i_out)
-    links.got(token_grad.at[other_rows, :], i_out + 1)
-
-    def last_waits(j, _):
+    for j in range(half_tiles):
         here = head_slot(j)
         rows = span(own_start + j * tile, tile)
         far_rows = span(sib_start + j * tile, tile)
+        for number, (rows_ref, out) in enumerate(
+            ((out_rows, block_out), (token_rows, token_grad))
+        ):
+            remote, local = finished(j, number, rows_ref, out)
+            remote.wait_send()
+            local.wait()
+            links.got(out.at[far_rows, :], i_out + number * half_tiles + j)
         links.sent(heads_own.at[rows, :], i_heads + j)
         links.sent(heads_own.at[far_rows, :], i_heads + half_tiles + j)
         links.sent(heads_own.at[far_rows, :], i_heads + 2 * half_tiles + j)
         links.sent(second_low.at[rows, :], i_second + j)
         links.sent(residual_low.at[rows, :], i_back + j)
         links.sent(second_sum.snd.at[here, :], second_sum.index + j)
-        for each in (second_sum, out_sum, first_sum):
+        for each in row_sums:
             links.sent(each.cs.at[here, :], each.index + half_tiles + j)
-        return 0
-
-    lax.fori_loop(0, half_tiles, last_waits, 0)
+
+
+def results_kernel(cols, hidden, blocks, down, up, output, qkv, vec, *outs):
+    (
+        query_out,
+        key_out,
+        value_out,
+        output_out,
+        up_out,
+        up_bias_out,
+        down_out,
+        *vectors,
+    ) = outs
+    for n, out in enumerate((query_out, key_out, value_out)):
+        out[...] = qkv[:, n * cols : (n + 1) * cols].astype(F32)
+    output_out[...] = output[...].astype(F32)
+    up_out[...] = up[...].astype(F32)
+    down_out[...] = down[...].astype(F32)
+
+    @pl.when(pl.program_id(0) == blocks - 1)
+    def _():
+        up_bias_out[...] = vec[6, 0:hidden]
+        for n, out in enumerate(vectors):
+            out[...] = vec[n, :]
 
 
 def kernel_shards(*args):
@@ -956,13 +1094,20 @@
     in_vmem = pl.BlockSpec(memory_space=pltpu.VMEM)
     scratch = [
         vmem((n_rows, width), BF16),
+        vmem((n_rows, width), BF16),
+        vmem((width, cols), BF16),
+        vmem((width, cols), BF16),
+        vmem((width, cols), BF16),
+        vmem((width, width), BF16),
+        vmem((width, hidden), BF16),
+        vmem((hidden, width), BF16),
+        vmem((n_rows, width), BF16),
         vmem((n_rows, cols), BF16),
         vmem((n_rows, cols), BF16),
         vmem((n_rows, cols), BF16),
         vmem((n_rows // tile * (cols // DH), tile, tile), F32),
         vmem((n_rows, cols), BF16),
         vmem((half, width), BF16),
-        vmem((width, width), BF16),
         vmem((half, width), F32),
         vmem((n_rows, width), BF16),
         vmem((n_rows, hidden), BF16),
@@ -983,7 +1128,7 @@
         vmem((8, width), F32),
         pltpu.SemaphoreType.DMA((N_SEMS,)),
         pltpu.SemaphoreType.DMA((N_SEMS,)),
-        pltpu.SemaphoreType.DMA((8,)),
+        pltpu.SemaphoreType.DMA((48,)),
     ]
     block_out, token_grad, down, up, output, qkv, vec = pl.pallas_call(
         functools.partial(layer_kernel, count),
@@ -993,7 +1138,7 @@
             *[jax.ShapeDtypeStruct(s, BF16) for s in grads],
             jax.ShapeDtypeStruct((8, width), F32),
         ],
-        in_specs=[in_vmem] * len(args),
+        in_specs=[any_space if a.ndim == 2 else in_vmem for a in args],
         out_specs=[any_space] * 6 + [in_vmem],
         scratch_shapes=scratch,
         compiler_params=pltpu.CompilerParams(
@@ -1001,22 +1146,35 @@
         ),
         name="layer",
     )(*args)
+
+    blocks = 4
+    by_rows = [pl.BlockSpec((r // blocks, n), lambda i: (i, 0)) for r, n in grads]
+    apart = pl.BlockSpec((width // blocks, cols), lambda i: (i, 0))
+    f32_grads = [jax.ShapeDtypeStruct(s, F32) for s in grads]
+    split = jax.ShapeDtypeStruct((width, cols), F32)
+    vector = jax.ShapeDtypeStruct((width,), F32)
+    query, key, value, output, up, up_bias, down, *vectors = pl.pallas_call(
+        functools.partial(results_kernel, cols, hidden, blocks),
+        grid=(blocks,),
+        out_shape=[split] * 3
+        + [f32_grads[2], f32_grads[1], jax.ShapeDtypeStruct((hidden,), F32), f32_grads[0]]
+        + [vector] * 6,
+        in_specs=by_rows + [in_vmem],
+        out_specs=[apart] * 3 + [by_rows[2], by_rows[1], in_vmem, by_rows[0]] + [in_vmem] * 6,
+        compiler_params=pltpu.CompilerParams(vmem_limit_bytes=48 * 2**20),
+        name="results",
+    )(down, up, output, qkv, vec)
     return (
         block_out,
         token_grad,
-        qkv[:, 0:cols].astype(F32),
-        qkv[:, cols : 2 * cols].astype(F32),
-        qkv[:, 2 * cols :].astype(F32),
-        output.astype(F32),
-        up.astype(F32),
-        vec[6, 0:hidden],
-        down.astype(F32),
-        vec[0],
-        vec[1],
-        vec[2],
-        vec[3],
-        vec[4],
-        vec[5],
+        query,
+        key,
+        value,
+        output,
+        up,
+        up_bias,
+        down,
+        *vectors,
     )
 
 

time: 181 us -> 127 us (0.70)
  Pallas kernels: 166 us -> 117 us
  other arithmetic: 7.43 us -> 0 us
  local copies, waits for them, and re-layouts: 5.26 us -> 9.17 us
    pallas_call x1, Pallas kernels: 166 us -> 113 us  [kernel_shards(): pl.pallas_call(functools.partial(layer_kernel, count), out_shape=[jax.Sha...]
    convert_element_type x4 -> x0, other arithmetic: 7.43 us -> none  [the longest x1 3.17 us: kernel_shards(): qkv[:, 2 * cols:].astype(F32)]
    unnamed x14 -> x16, local copies, waits for them, and re-layouts: 4.05 us -> 9.17 us
    pallas_call x0 -> x1, Pallas kernels: none -> 3.6 us  [kernel_shards(): pl.pallas_call(functools.partial(results_kernel, cols, hidden, blocks), g...]
where the time goes in v2:
time: 127 us
  Pallas kernels  117 us (92%)
  local copies, waits for them, and re-layouts  9.17 us (7%)
    pallas_call x1, Pallas kernels, kernel_shards(): pl.pallas_call(functools.partial(layer_kernel, count), out_shape=[jax.Sha...  113 us
    unnamed x16, local copies, waits for them, and re-layouts  9.17 us
    pallas_call x1, Pallas kernels, kernel_shards(): pl.pallas_call(functools.partial(results_kernel, cols, hidden, blocks), g...  3.6 us

profile of v2, /device:TPU:0, one launch (start us, length us, event | category | flops | bytes accessed | tf_op | source)
XLA Modules:
  0.0 126.6 jit_solution(2646719361862362592)
XLA Ops:
  0.7 113.1 %layer.1 = (bf16[960,1024]{1,0:T(8,128)(2,1)}, bf16[960,1024]{1,0:T(8,128)(2,1)}, bf16[512,1024]{1,0:T(8,128)(2,1)}, bf16[1024,512]{1,0:T(8,128)(2,1)}, bf16[256...) custom-call(bf16[960,1024]{1,0:T(8,128)(2,1)} %tokens_hbm.1, s32[64]{0:T(128)} %lengths.1, ...), custom_call_target="tpu_custom_call" | custom-call | tf_op jit(solution)/shard_map/layer/pallas_call | solution.py:1133
  113.8 0.0 copy-start
  113.8 1.4 %copy-done = bf16[1024,768]{1,0:T(8,128)(2,1)S(1)} copy-done((bf16[1024,768]{1,0:T(8,128)(2,1)S(1)}, bf16[1024,768]{1,0:T(8,128)(2,1)}, u32[]{:S(2)}) %copy-start) | copy-done | bytes 1572888
  115.2 0.0 copy-start.1
  115.2 1.2 copy-done.1
  116.4 0.0 copy-start.2
  116.4 1.2 copy-done.2
  117.6 0.0 copy-start.3
  117.6 1.0 copy-done.3
  118.7 0.0 copy-start.4
  118.7 0.8 copy-done.4
  119.4 0.0 copy-start.6
  119.4 3.6 %results.1 = (f32[1024,256]{1,0:T(8,128)}, f32[1024,256]{1,0:T(8,128)}, f32[1024,256]{1,0:T(8,128)}, f32[256,1024]{1,0:T(8,128)}, f32[1024,512]{1,0:T(8,128)}, /...) custom-call(bf16[512,1024]{1,0:T(8,128)(2,1)S(1)} %copy-done.1, ...), custom_call_target="tpu_custom_call" | custom-call | tf_op jit(solution)/shard_map/results/pallas_call | solution.py:1156
  123.0 0.0 copy-done.6
  123.0 0.0 copy-start.5
  123.1 1.3 %copy.33 = bf16[960,1024]{1,0:T(8,128)(2,1)} copy(bf16[960,1024]{1,0:T(8,128)(2,1)S(1)} %copy-done.6) | data formatting | bytes 3932160
  124.3 1.0 copy-done.5
  125.3 1.3 %copy.34 = bf16[960,1024]{1,0:T(8,128)(2,1)} copy(bf16[960,1024]{1,0:T(8,128)(2,1)S(1)} %copy-done.5) | data formatting | bytes 3932160
Async XLA Ops:
  113.8 1.4 %copy-start = (bf16[1024,768]{1,0:T(8,128)(2,1)S(1)}, bf16[1024,768]{1,0:T(8,128)(2,1)}, u32[]{:S(2)}) copy-start(bf16[1024,768]{1,0:T(8,128)(2,1)} %get-tuple-element.40.qkv) | copy-start | bytes 4718596
  115.2 1.2 copy-start.1
  116.4 1.2 copy-start.2
  117.6 1.0 copy-start.3
  118.7 0.8 copy-start.4
  119.4 3.6 %copy-start.6 = (bf16[960,1024]{1,0:T(8,128)(2,1)S(1)}, bf16[960,1024]{1,0:T(8,128)(2,1)}, u32[]{:S(2)}) copy-start(bf16[960,1024]{1,0:T(8,128)(2,1)} %get-tuple-element.70) | copy-start | bytes 5898244
  123.0 2.3 %copy-start.5 = (bf16[960,1024]{1,0:T(8,128)(2,1)S(1)}, bf16[960,1024]{1,0:T(8,128)(2,1)}, u32[]{:S(2)}) copy-start(bf16[960,1024]{1,0:T(8,128)(2,1)} %get-tuple-element.71) | copy-start | bytes 5898244

commit v3 on v2

--- a/solution.py
+++ b/solution.py
@@ -261,26 +261,28 @@
 F32 = jnp.float32
 BF16 = jnp.bfloat16
 MESH = pl.DeviceIdType.MESH
-N_SEMS = 192
+N_SENDS = 32
+N_RECVS = 128
+N_LOCAL = 19
 
 PARTS = (
-    ("D", 0, 128, "a"), ("D", 128, 128, "d"), ("D", 256, 128, "d"), ("D", 384, 128, "a"),
-    ("U", 0, 256, "a"), ("U", 256, 256, "d"), ("U", 512, 256, "a"), ("U", 768, 256, "a"),
-    ("O", 0, 128, "a"), ("O", 128, 128, "a"), ("Q", 0, 128, "d"), ("Q", 128, 128, "d"),
-    ("Q", 256, 128, "a"), ("Q", 384, 128, "d"), ("Q", 512, 128, "a"), ("Q", 640, 128, "a"),
-    ("Q", 768, 128, "a"), ("Q", 896, 128, "d"),
+    ("D", 0, 128, "d"), ("D", 128, 128, "a"), ("D", 256, 128, "a"), ("D", 384, 128, "a"),
+    ("U", 0, 256, "d"), ("U", 256, 256, "d"), ("U", 512, 256, "a"), ("U", 768, 256, "a"),
+    ("O", 0, 128, "a"), ("O", 128, 128, "a"), ("Q", 0, 128, "a"), ("Q", 128, 128, "d"),
+    ("Q", 256, 128, "a"), ("Q", 384, 128, "a"), ("Q", 512, 128, "d"), ("Q", 640, 128, "d"),
+    ("Q", 768, 128, "d"), ("Q", 896, 128, "a"),
 )
 ORDER = (
-    "U1", "S0", "D0", "S1", "D1", "V0", "T0", "U3", "T1", "U0", "5.1", "W0", "U2", "0.1", "V1",
-    "1.1", "3.1", "5.2", "2.1", "7.1", "1.2", "0.2", "4.1", "e5.3", "2.2", "B0", "3.2", "6.1",
-    "e1.3", "A0", "7.2", "0.3", "A1", "e2.3", "e5.4", "F0", "e1.4", "4.2", "3.3", "G0", "e0.4",
-    "e2.4", "6.2", "7.3", "B1", "e3.4", "5.5", "4.3", "A2", "A3", "e7.4", "6.3", "1.5", "Q1", "O0",
-    "e4.4", "Q3", "2.5", "5.6", "F1", "Q0", "Q2", "e6.4", "13.1", "1.6", "G1", "W1", "X0", "17.1",
-    "12.1", "2.6", "10.1", "8.1", "13.2", "11.1", "17.2", "9.1", "e13.3", "12.2", "10.2", "16.1",
-    "e17.3", "8.2", "Y0", "11.2", "14.1", "e10.3", "12.3", "9.2", "15.1", "e11.3", "e12.4",
-    "e13.4", "e8.4", "8.3", "16.2", "14.2", "9.3", "15.2", "16.3", "Y1", "Z0", "e17.4", "e9.4",
-    "14.3", "Z1", "e10.4", "e16.4", "e11.4", "e14.4", "13.5", "15.3", "17.5", "13.6", "Z2",
-    "e15.4", "10.5", "17.6", "X1", "11.5", "10.6", "11.6",
+    "P0", "E0", "P1", "E2", "E1", "V0", "S0", "E3", "U0", "D0", "S1", "U3", "T0", "D1", "U2", "T1",
+    "V1", "U1", "W0", "4.1", "1.1", "0.1", "7.1", "4.2", "5.1", "2.1", "e4.3", "0.2", "1.2", "3.1",
+    "B0", "5.2", "A0", "e0.3", "7.2", "6.1", "A1", "1.3", "F0", "e5.3", "e4.4", "2.2", "G0",
+    "e1.4", "e0.4", "7.3", "3.2", "2.3", "6.2", "B1", "e5.4", "e7.4", "A2", "3.3", "4.5", "A3",
+    "e2.4", "Q2", "6.3", "O0", "Q3", "Q0", "0.5", "F1", "e3.4", "Q1", "4.6", "5.5", "G1", "W1",
+    "e6.4", "0.6", "14.1", "X0", "8.1", "15.1", "5.6", "16.1", "9.1", "14.2", "11.1", "17.1",
+    "15.2", "10.1", "e14.3", "e15.3", "16.2", "8.2", "12.1", "e16.3", "Y0", "11.2", "9.2", "13.1",
+    "e11.3", "e8.4", "e14.4", "e9.4", "8.3", "17.2", "10.2", "9.3", "12.2", "17.3", "13.2", "10.3",
+    "Y1", "Z0", "e15.4", "e17.4", "12.3", "Z1", "e16.4", "e10.4", "e11.4", "14.5", "13.3", "15.5",
+    "14.6", "Z2", "e12.4", "e13.4", "16.5", "15.6", "11.5", "X1", "16.6", "11.6",
 )
 
 
@@ -307,48 +309,53 @@
 class Links:
     def __init__(self, sends, recvs, anyone):
         self.sends, self.recvs, self.anyone = sends, recvs, anyone
-        self.used = 0
+        self.used = [0, 0]
+
+    def group(self):
+        self.used[0] += 1
+        assert self.used[0] <= N_SENDS
+        return self.used[0] - 1
 
     def take(self, count=1):
-        first = self.used
-        self.used += count
-        assert self.used <= N_SEMS
+        first = self.used[1]
+        self.used[1] += count
+        assert self.used[1] <= N_RECVS
         return first
 
-    def copy(self, src, dst, index, device):
+    def copy(self, src, dst, group, index, device):
         return pltpu.make_async_remote_copy(
             src_ref=src,
             dst_ref=dst,
-            send_sem=self.sends.at[index],
+            send_sem=self.sends.at[group],
             recv_sem=self.recvs.at[index],
             device_id=device,
             device_id_type=MESH,
         )
 
     def got(self, dst, index):
-        self.copy(dst, dst, index, self.anyone).wait_recv()
-
-    def sent(self, src, index):
-        self.copy(src, src, index, self.anyone).wait_send()
+        self.copy(dst, dst, 0, index, self.anyone).wait_recv()
+
+    def sent(self, like, group):
+        self.copy(like, like, group, 0, self.anyone).wait_send()
 
 
 def layer_kernel(
     count,
     tokens_hbm,
-    lengths,
+    lengths_hbm,
     query_hbm,
     key_hbm,
     value_hbm,
     output_hbm,
     up_hbm,
-    up_bias,
+    up_bias_hbm,
     down_hbm,
-    first_gain,
-    first_shift,
-    second_gain,
-    second_shift,
-    output_bias,
-    down_bias,
+    first_gain_hbm,
+    first_shift_hbm,
+    second_gain_hbm,
+    second_shift_hbm,
+    output_bias_hbm,
+    down_bias_hbm,
     cotangent_hbm,
     block_out,
     token_grad,
@@ -357,6 +364,14 @@
     output_out,
     qkv_out,
     vec_out,
+    lengths,
+    up_bias,
+    first_gain,
+    first_shift,
+    second_gain,
+    second_shift,
+    output_bias,
+    down_bias,
     tokens,
     cotangent,
     query_weight,
@@ -396,15 +411,10 @@
     rm_up,
     rm_output,
     rm_qkv,
-    t_down,
-    t_up,
-    t_output,
-    t_qkv,
     vec,
     vec_sib,
     vec_parts,
     vec_sum,
-    vec_all,
     sends,
     recvs,
     local_sems,
@@ -444,7 +454,6 @@
     for peer in [sib, opp, diag] + dp_peers:
         pl.semaphore_signal(barrier, inc=1, device_id=peer, device_id_type=MESH)
 
-    own_rows = span(c * half, half)
     other_rows = span((1 - c) * half, half)
     own_start = c * half
     sib_start = (1 - c) * half
@@ -464,7 +473,15 @@
                 (query_hbm, query_weight),
                 (key_hbm, key_weight),
                 (value_hbm, value_weight),
+                (lengths_hbm, lengths),
+                (first_gain_hbm, first_gain),
+                (first_shift_hbm, first_shift),
                 (output_hbm, wo_all.at[own_wo, :]),
+                (output_bias_hbm, output_bias),
+                (second_gain_hbm, second_gain),
+                (second_shift_hbm, second_shift),
+                (up_bias_hbm, up_bias),
+                (down_bias_hbm, down_bias),
                 (up_hbm, up_weight),
                 (down_hbm, down_weight),
                 (cotangent_hbm, cotangent),
@@ -472,13 +489,13 @@
         )
     ]
     token_load(0).start()
-    for load in loads[:3]:
+    early = 6
+    for load in loads[:early]:
         load.start()
     for i in range(1, n_tiles):
         token_load(i).start()
-    for load in loads[3:]:
+    for load in loads[early:]:
         load.start()
-    free_sem = n_tiles + len(loads)
 
     def row(ref):
         return ref[...].astype(F32).reshape(1, ref.shape[0])
@@ -494,45 +511,53 @@
     def wo_piece(owner, number):
         return wo_all.at[span(owner * cols + number * piece, piece), :]
 
-    i_wo = links.take(9)
+    i_wo = links.take(7)
+    s_wo = links.group()
     by_y = links.copy(
-        output_hbm.at[span(quarter * piece, piece), :], wo_piece(t, quarter), i_wo, opp
-    )
-    whole_to_sib = links.copy(output_hbm, wo_all.at[own_wo, :], i_wo + 1, sib)
+        output_hbm.at[span(quarter * piece, piece), :], wo_piece(t, quarter), s_wo, i_wo, opp
+    )
+    whole_to_sib = links.copy(output_hbm, wo_all.at[own_wo, :], s_wo, i_wo + 1, sib)
     q_xp, q_adj = quarter + 1 - 2 * x, quarter + 2 - 4 * (z % 2)
     q_cross = q_adj + 1 - 2 * x
     mine = wo_piece(t_opp, quarter)
-    to_x = links.copy(mine, mine, i_wo + 2, xp)
-    to_z = links.copy(mine, mine, i_wo + 3, adj)
-    from_x = wo_piece(t_opp, q_xp)
-    on_z = links.copy(from_x, from_x, i_wo + 4, adj)
-    others = ((quarter, None), (q_xp, i_wo + 2), (q_adj, i_wo + 3), (q_cross, i_wo + 4))
-    relays = [
-        links.copy(wo_piece(t_opp, q), wo_piece(t_opp, q), i_wo + 5 + n, sib)
-        for n, (q, _i) in enumerate(others)
-    ]
+    to_x = links.copy(mine, mine, s_wo, i_wo + 2, xp)
+    to_z = links.copy(mine, mine, s_wo, i_wo + 3, adj)
+
+    def half_piece(number, which):
+        return wo_all.at[span(t_opp * cols + number * piece + which * piece // 2, piece // 2), :]
+
+    from_x, from_z = half_piece(q_xp, 0), half_piece(q_adj, 1)
+    on_z = links.copy(from_x, from_x, s_wo, i_wo + 4, adj)
+    on_x = links.copy(from_z, from_z, s_wo, i_wo + 5, xp)
+
+    def relay(number):
+        part = wo_piece(t_opp, number)
+        links.copy(part, part, s_wo, i_wo + 6, sib).start()
 
     def share_first():
         links.got(mine, i_wo)
         to_x.start()
         to_z.start()
-        relays[0].start()
+        relay(quarter)
 
     def share_next():
-        links.got(from_x, i_wo + 2)
+        links.got(wo_piece(t_opp, q_xp), i_wo + 2)
         on_z.start()
-        relays[1].start()
+        links.got(wo_piece(t_opp, q_adj), i_wo + 3)
+        on_x.start()
+        relay(q_xp)
+        relay(q_adj)
 
     def share_last():
-        links.got(wo_piece(t_opp, q_adj), i_wo + 3)
-        relays[2].start()
-        links.got(wo_piece(t_opp, q_cross), i_wo + 4)
-        relays[3].start()
+        links.got(half_piece(q_cross, 0), i_wo + 4)
+        links.got(half_piece(q_cross, 1), i_wo + 5)
+        relay(q_cross)
         links.got(wo_all.at[span(t_sib * cols, cols), :], i_wo + 1)
-        for n, q in enumerate((quarter, q_xp, q_adj, q_cross)):
-            links.got(wo_piece(t_diag, q), i_wo + 5 + n)
-
-    wo_sends = [by_y, whole_to_sib, to_x, to_z, on_z] + relays
+        links.got(wo_all.at[span(t_diag * cols, cols), :], i_wo + 6)
+
+    pl.semaphore_wait(barrier, 10)
+    by_y.start()
+    whole_to_sib.start()
 
     def allowed_of(number):
         def series_of(index):
@@ -553,7 +578,8 @@
         seen = jnp.logical_and(live, col_at <= row_at)
         return jnp.logical_and(same, jnp.logical_or(seen, col_at == row_at))
 
-    i_heads = links.take(3 * half_tiles)
+    i_heads = links.take(half_tiles)
+    s_heads = links.group()
 
     def head_slot(j):
         return span(j * tile, tile)
@@ -563,13 +589,14 @@
         number = h * half_tiles + j
         rows = turn_rows(i)
         token_load(i).wait()
+
+        @pl.when(i == 0)
+        def _():
+            for load in loads[:early]:
+                load.wait()
+
         xhat, _r = norm_parts(tokens[rows, :].astype(F32))
         first_low[rows, :] = (xhat * row(first_gain) + row(first_shift)).astype(BF16)
-
-        @pl.when(i == 0)
-        def _():
-            for load in loads[:3]:
-                load.wait()
 
         normed = first_low[rows, :]
         q = dot(normed, query_weight[...]).astype(BF16)
@@ -578,12 +605,6 @@
         queries[rows, :] = q
         key_rows[rows, :] = k
         value_rows[rows, :] = v
-
-        @pl.when(i == 0)
-        def _():
-            pl.semaphore_wait(barrier, 10)
-            by_y.start()
-            whole_to_sib.start()
 
         allowed = allowed_of(number)
         for head in range(heads_here):
@@ -598,14 +619,14 @@
         @pl.when(h == c)
         def _():
             heads_full[head_slot(j), lanes(t * cols, cols)] = heads_own[rows, :]
-            links.copy(heads_own.at[rows, :], slot, i_heads + j, opp).start()
+            links.copy(heads_own.at[rows, :], slot, s_heads, i_heads + j, opp).start()
 
         @pl.when(h != c)
         def _():
-            links.copy(heads_own.at[rows, :], slot, i_heads + half_tiles + j, sib).start()
-            links.copy(heads_own.at[rows, :], slot, i_heads + 2 * half_tiles + j, diag).start()
-
-        @pl.when(i == 3)
+            links.copy(heads_own.at[rows, :], slot, s_heads, i_heads + j, sib).start()
+            links.copy(heads_own.at[rows, :], slot, s_heads, i_heads + j, diag).start()
+
+        @pl.when(i == 1)
         def _():
             share_first()
 
@@ -614,11 +635,9 @@
     lax.fori_loop(0, n_tiles, attend, 0)
 
     share_next()
-    for load in loads[3:]:
-        load.wait()
-    share_last()
 
     i_second = links.take(half_tiles)
+    s_second = links.group()
     vec[...] = jnp.zeros_like(vec)
 
     def in_turn(i):
@@ -626,6 +645,8 @@
 
     def feed(i):
         rows = span(in_turn(i), tile)
+        if i % 2 == 1:
+            links.got(second_low.at[rows, :], i_second + i // 2)
         u = dot(second_low[rows, :], up_weight[...]) + row(up_bias)
         big = 0.5 * (1.0 + lax.erf(u * (1.0 / math.sqrt(2.0))))
         act[rows, :] = (u * big).astype(BF16)
@@ -634,69 +655,61 @@
         ugp[rows, :] = grad
         vec[6:7, 0:hidden] += jnp.sum(grad.astype(F32), axis=0, keepdims=True)
 
-    def project(j, _):
+    def project(j):
+        if j == 0:
+            for load in loads[early:]:
+                load.wait()
+            share_last()
         here = head_slot(j)
-        for n, who in enumerate((t_opp, t_sib, t_diag)):
-            links.got(heads_full.at[here, lanes(who * cols, cols)], i_heads + n * half_tiles + j)
+        links.got(heads_full.at[here, 0 : 3 * cols], i_heads + j)
         rows = span(own_start + j * tile, tile)
         v = tokens[rows, :].astype(F32) + dot(heads_full[here, :], wo_all[...]) + row(output_bias)
         residual[here, :] = v
         xhat, _r = norm_parts(v)
         second_low[rows, :] = (xhat * row(second_gain) + row(second_shift)).astype(BF16)
-        links.copy(second_low.at[rows, :], second_low.at[rows, :], i_second + j, sib).start()
-        feed(2 * j)
-        links.got(second_low.at[span(sib_start + j * tile, tile), :], i_second + j)
-        feed(2 * j + 1)
-        return 0
-
-    lax.fori_loop(0, half_tiles, project, 0)
+        links.copy(
+            second_low.at[rows, :], second_low.at[rows, :], s_second, i_second + j, sib
+        ).start()
 
     class Tensor:
-        def __init__(self, grads, rx, rz, rm, total, out):
-            self.grads, self.rx, self.rz, self.rm, self.total, self.out = (
-                grads, rx, rz, rm, total, out,
-            )
+        def __init__(self, grads, rx, rz, rm, out):
+            self.grads, self.rx, self.rz, self.rm, self.out = grads, rx, rz, rm, out
 
     tensors = {
-        "D": Tensor(g_down, rx_down, rz_down, rm_down, t_down, down_out),
-        "U": Tensor(g_up, rx_up, rz_up, rm_up, t_up, up_out),
-        "O": Tensor(g_output, rx_output, rz_output, rm_output, t_output, output_out),
-        "Q": Tensor(g_qkv, rx_qkv, rz_qkv, rm_qkv, t_qkv, qkv_out),
+        "D": Tensor(g_down, rx_down, rz_down, rm_down, down_out),
+        "U": Tensor(g_up, rx_up, rz_up, rm_up, up_out),
+        "O": Tensor(g_output, rx_output, rz_output, rm_output, output_out),
+        "Q": Tensor(g_qkv, rx_qkv, rz_qkv, rm_qkv, qkv_out),
     }
 
     class Part:
-        def __init__(self, tensor, start, size, sem):
+        def __init__(self, tensor, start, size):
             self.size = size // 2
             self.start = start
             here = pl.ds(start // 2, self.size)
             self.grads, self.out = tensor.grads, tensor.out
-            self.rx, self.rz, self.rm, self.total = (
-                ref.at[here, :] for ref in (tensor.rx, tensor.rz, tensor.rm, tensor.total)
+            self.rx, self.rz, self.rm = (
+                ref.at[here, :] for ref in (tensor.rx, tensor.rz, tensor.rm)
             )
-            self.index = links.take(self.messages)
-            self.sem = sem
+            self.index = links.take(4)
+            self.group = links.group()
 
         def half_at(self, which):
             return span(self.start + which * self.size, self.size)
 
         def send(self, src, dst, message, device):
-            links.copy(src, dst, self.index + message, device).start()
+            links.copy(src, dst, self.group, self.index + message, device).start()
 
         def got(self, dst, message):
             links.got(dst, self.index + message)
 
-        def sent(self, src, message):
-            links.sent(src, self.index + message)
-
         def add(self, rows, came):
             return (self.grads[rows, :].astype(F32) + came[...].astype(F32)).astype(BF16)
 
-        def write(self, rows):
-            return pltpu.make_async_copy(self.total, self.out.at[rows, :], local_sems.at[self.sem])
+        def sent(self, copies):
+            links.sent(self.grads.at[0 : copies * self.size, :], self.group)
 
     class PartX(Part):
-        messages = 5
-
         def begin(self):
             self.send(self.grads.at[self.half_at(1 - x), :], self.rx, 0, xp)
 
@@ -724,39 +737,29 @@
                 @pl.when(is_mid)
                 def _():
                     self.got(self.rm, 2)
-                    self.total[...] = self.add(mine, self.rm)
-                    self.send(self.total, out, 3, adj)
-                    self.send(self.total, out, 4, xp)
-                    self.write(mine).start()
+                    self.out[mine, :] = self.add(mine, self.rm)
+                    self.send(out, out, 1, adj)
+                    self.send(out, out, 3, xp)
 
             if number == 4:
 
                 @pl.when(is_end)
                 def _():
-                    self.got(out, 3)
-                    self.send(out, out, 4, xp)
+                    self.got(out, 1)
+                    self.send(out, out, 3, xp)
 
         def end(self):
-            mine, other = self.half_at(x), self.half_at(1 - x)
-            grads, out = self.grads.at[mine, :], self.out.at[mine, :]
-            self.sent(self.grads.at[other, :], 0)
-            self.got(self.out.at[other, :], 4)
+            self.got(self.out.at[self.half_at(1 - x), :], 3)
 
             @pl.when(is_end)
             def _():
-                self.sent(grads, 1)
-                self.sent(out, 4)
+                self.sent(3)
 
             @pl.when(is_mid)
             def _():
-                self.sent(grads, 2)
-                self.sent(self.total, 3)
-                self.sent(self.total, 4)
-                self.write(mine).wait()
+                self.sent(4)
 
     class PartZ(Part):
-        messages = 7
-
         def begin(self):
             far = self.grads.at[self.half_at(1 - side), :]
 
@@ -776,44 +779,37 @@
                 if number == 2:
                     self.got(self.rm, 1)
                     self.grads[near, :] = self.add(near, self.rm)
-                    self.send(self.grads.at[near, :], self.rz, 2, adj)
+                    self.send(self.grads.at[near, :], self.rz, 0, adj)
                 if number == 3:
-                    self.got(self.rz, 2)
+                    self.got(self.rz, 0)
                     self.grads[near, :] = self.add(near, self.rz)
-                    self.send(self.grads.at[near, :], self.rx, 3, xp)
+                    self.send(self.grads.at[near, :], self.rx, 1, xp)
                 if number == 4:
-                    self.got(self.rx, 3)
-                    self.total[...] = self.add(near, self.rx)
-                    self.send(self.total, self.out.at[near, :], 4, adj)
-                    self.write(near).start()
+                    self.got(self.rx, 1)
+                    self.out[near, :] = self.add(near, self.rx)
+                    self.send(self.out.at[near, :], self.out.at[near, :], 2, adj)
                 if number == 5:
-                    self.got(self.out.at[near, :], 4)
-                    self.send(self.out.at[near, :], self.out.at[near, :], 5, mid)
+                    self.got(self.out.at[near, :], 2)
+                    self.send(self.out.at[near, :], self.out.at[near, :], 3, mid)
                 if number == 6:
-                    self.got(self.out.at[far, :], 5)
-                    self.send(self.out.at[far, :], self.out.at[far, :], 6, adj)
+                    self.got(self.out.at[far, :], 3)
+                    self.send(self.out.at[far, :], self.out.at[far, :], 2, adj)
 
         def end(self):
             near, far = self.half_at(side), self.half_at(1 - side)
 
             @pl.when(is_end)
             def _():
-                self.got(self.out.at[far, :], 6)
-                self.sent(self.grads.at[far, :], 0)
-                self.sent(self.grads.at[near, :], 3)
-                self.sent(self.total, 4)
-                self.write(near).wait()
+                self.got(self.out.at[far, :], 2)
+                self.sent(3)
 
             @pl.when(is_mid)
             def _():
-                self.sent(self.grads.at[far, :], 1)
-                self.sent(self.grads.at[near, :], 2)
-                self.sent(self.out.at[near, :], 5)
-                self.sent(self.out.at[far, :], 6)
+                self.sent(4)
 
     parts = [
-        {"a": PartX, "d": PartZ}[kind](tensors[name], start, size, free_sem + n)
-        for n, (name, start, size, kind) in enumerate(PARTS)
+        {"a": PartX, "d": PartZ}[kind](tensors[name], start, size)
+        for name, start, size, kind in PARTS
     ]
 
     def begin_parts(name, first, size):
@@ -847,11 +843,14 @@
             self.snd, self.r1, self.cs, self.r2 = (mail.at[4 * number + n] for n in range(4))
             self.part = part
             self.index = links.take(2 * half_tiles)
+            self.group = links.group()
 
         def far(self, j):
             here = head_slot(j)
             self.snd[here, :] = self.part(span(sib_start + j * tile, tile)).astype(BF16)
-            links.copy(self.snd.at[here, :], self.r1.at[here, :], self.index + j, sib).start()
+            links.copy(
+                self.snd.at[here, :], self.r1.at[here, :], self.group, self.index + j, sib
+            ).start()
 
         def near(self, j):
             here = head_slot(j)
@@ -859,7 +858,11 @@
             links.got(self.r1.at[here, :], self.index + j)
             self.cs[here, :] = (mine + self.r1[here, :].astype(F32)).astype(BF16)
             links.copy(
-                self.cs.at[here, :], self.r2.at[here, :], self.index + half_tiles + j, opp
+                self.cs.at[here, :],
+                self.r2.at[here, :],
+                self.group,
+                self.index + half_tiles + j,
+                opp,
             ).start()
 
         def rows(self, j):
@@ -867,10 +870,8 @@
             links.got(self.r2.at[here, :], self.index + half_tiles + j)
             return self.cs[here, :].astype(F32) + self.r2[here, :].astype(F32)
 
-        def end(self, j):
-            here = head_slot(j)
-            links.sent(self.snd.at[here, :], self.index + j)
-            links.sent(self.cs.at[here, :], self.index + half_tiles + j)
+        def end(self):
+            links.sent(first_low, self.group)
 
     second_sum = RowSum(0, lambda rows: dot_nt(ugp[rows, :], up_weight[...]))
     out_sum = RowSum(1, lambda rows: dot(act[rows, :], down_weight[...]))
@@ -883,6 +884,7 @@
     row_sums = (second_sum, out_sum, first_sum)
 
     i_back = links.take(half_tiles)
+    s_back = links.group()
 
     def add_to(at, value):
         vec[at : at + 1, :] += jnp.sum(value, axis=0, keepdims=True)
@@ -904,7 +906,9 @@
         grad = given + norm_back(incoming, xhat, r, row(second_gain))
         residual_grad[local, :] = grad
         residual_low[rows, :] = grad.astype(BF16)
-        links.copy(residual_low.at[rows, :], residual_low.at[rows, :], i_back + j, sib).start()
+        links.copy(
+            residual_low.at[rows, :], residual_low.at[rows, :], s_back, i_back + j, sib
+        ).start()
         add_to(2, incoming * xhat)
         add_to(3, incoming)
         add_to(4, grad)
@@ -934,26 +938,17 @@
                 share.astype(BF16), grads[:, at]
             ).astype(BF16)
 
-    i_out = links.take(2 * half_tiles)
-    out_rows = mail.at[4]
-    token_rows = mail.at[8]
-    out_sem = free_sem + len(PARTS)
-
-    def finished(j, number, rows_ref, out):
+    i_out = links.take(2)
+    s_out = links.group()
+
+    def finished(j, number, out, values):
         rows = span(own_start + j * tile, tile)
-        src = rows_ref.at[head_slot(j), :]
-        n = number * half_tiles + j
-        return (
-            links.copy(src, out.at[rows, :], i_out + n, sib),
-            pltpu.make_async_copy(src, out.at[rows, :], local_sems.at[out_sem + n]),
-        )
+        out[rows, :] = values.astype(BF16)
+        links.copy(out.at[rows, :], out.at[rows, :], s_out, i_out + number, sib).start()
 
     def finish_out(j):
         local = head_slot(j)
-        links.sent(out_sum.snd.at[local, :], out_sum.index + j)
-        out_rows[local, :] = (residual[local, :] + out_sum.rows(j) + row(down_bias)).astype(BF16)
-        for each in finished(j, 0, out_rows, block_out):
-            each.start()
+        finished(j, 0, block_out, residual[local, :] + out_sum.rows(j) + row(down_bias))
 
     def first_back(j):
         local = head_slot(j)
@@ -961,47 +956,44 @@
         incoming = first_sum.rows(j)
         xhat, r = norm_parts(tokens[rows, :].astype(F32))
         grad = residual_grad[local, :] + norm_back(incoming, xhat, r, row(first_gain))
-        links.sent(first_sum.snd.at[local, :], first_sum.index + j)
-        token_rows[local, :] = grad.astype(BF16)
-        for each in finished(j, 1, token_rows, token_grad):
-            each.start()
+        finished(j, 1, token_grad, grad)
         add_to(0, incoming * xhat)
         add_to(1, incoming)
 
-    i_vec = links.take(1 + 2 * 7)
-    vec_send = links.copy(vec, vec_sib, i_vec, sib)
+    i_vec = links.take(3)
+    s_vec = [links.group() for _ in range(3)]
     part = width // 8
     mine_at = lanes(dp * part, part)
-    part_sends = [
-        links.copy(vec.at[:, lanes(peer[0] * part, part)], vec_parts.at[dp], i_vec + 1 + k, peer)
-        for k, peer in enumerate(dp_peers)
-    ]
-    sum_sends = [
-        links.copy(vec_sum, vec_all.at[:, mine_at], i_vec + 8 + k, peer)
-        for k, peer in enumerate(dp_peers)
-    ]
+    seven = vec_parts.at[0:7]
 
     def vectors(number):
         if number == 0:
-            vec_send.start()
+            links.copy(vec, vec_sib, s_vec[0], i_vec, sib).start()
         if number == 1:
             links.got(vec_sib, i_vec)
-            vec_send.wait_send()
+            links.sent(vec, s_vec[0])
             at_row = lax.broadcasted_iota(jnp.int32, vec.shape, 0)
             vec[...] = vec[...] + jnp.where(at_row < 6, vec_sib[...], 0.0)
             vec_parts[dp] = vec[:, mine_at]
-            for send in part_sends:
-                send.start()
+            for peer in dp_peers:
+                links.copy(
+                    vec.at[:, lanes(peer[0] * part, part)],
+                    vec_parts.at[dp],
+                    s_vec[1],
+                    i_vec + 1,
+                    peer,
+                ).start()
         if number == 2:
-            for k in range(7):
-                links.got(vec_parts.at[(dp + 7 - k) % 8], i_vec + 1 + k)
+            links.got(seven, i_vec + 1)
             total = vec_parts[0]
             for k in range(1, 8):
                 total = total + vec_parts[k]
             vec_sum[...] = total
-            vec_all[:, mine_at] = total
-            for send in sum_sends:
-                send.start()
+            vec_out[:, mine_at] = total
+            for peer in dp_peers:
+                links.copy(vec_sum, vec_out.at[:, mine_at], s_vec[2], i_vec + 2, peer).start()
+        if number == 3:
+            links.got(seven, i_vec + 2)
 
     tasks = {
         "D": down_grads,
@@ -1019,6 +1011,8 @@
         "X": finish_out,
         "Y": first_back,
         "Z": vectors,
+        "P": project,
+        "E": feed,
     }
     for name in ORDER:
         if "." in name:
@@ -1027,56 +1021,43 @@
         else:
             tasks[name[0]](int(name[1:]))
 
-    for k in range(7):
-        links.got(vec_all.at[:, lanes(((dp + 7 - k) % 8) * part, part)], i_vec + 8 + k)
-    vec_out[...] = vec_all[...]
+    vectors(3)
+
     for each in parts:
         each.end()
-    for send in wo_sends + part_sends + sum_sends:
-        send.wait_send()
-    for j in range(half_tiles):
-        here = head_slot(j)
-        rows = span(own_start + j * tile, tile)
-        far_rows = span(sib_start + j * tile, tile)
-        for number, (rows_ref, out) in enumerate(
-            ((out_rows, block_out), (token_rows, token_grad))
-        ):
-            remote, local = finished(j, number, rows_ref, out)
-            remote.wait_send()
-            local.wait()
-            links.got(out.at[far_rows, :], i_out + number * half_tiles + j)
-        links.sent(heads_own.at[rows, :], i_heads + j)
-        links.sent(heads_own.at[far_rows, :], i_heads + half_tiles + j)
-        links.sent(heads_own.at[far_rows, :], i_heads + 2 * half_tiles + j)
-        links.sent(second_low.at[rows, :], i_second + j)
-        links.sent(residual_low.at[rows, :], i_back + j)
-        links.sent(second_sum.snd.at[here, :], second_sum.index + j)
-        for each in row_sums:
-            links.sent(each.cs.at[here, :], each.index + half_tiles + j)
-
-
-def results_kernel(cols, hidden, blocks, down, up, output, qkv, vec, *outs):
-    (
-        query_out,
-        key_out,
-        value_out,
-        output_out,
-        up_out,
-        up_bias_out,
-        down_out,
-        *vectors,
-    ) = outs
-    for n, out in enumerate((query_out, key_out, value_out)):
-        out[...] = qkv[:, n * cols : (n + 1) * cols].astype(F32)
-    output_out[...] = output[...].astype(F32)
-    up_out[...] = up[...].astype(F32)
-    down_out[...] = down[...].astype(F32)
-
-    @pl.when(pl.program_id(0) == blocks - 1)
-    def _():
-        up_bias_out[...] = vec[6, 0:hidden]
-        for n, out in enumerate(vectors):
-            out[...] = vec[n, :]
+    links.sent(wo_all.at[0 : 3 * cols, :], s_wo)
+    links.sent(heads_full.at[:, 0 : 3 * cols], s_heads)
+    links.sent(second_low.at[0:half, :], s_second)
+    links.sent(residual_low.at[0:half, :], s_back)
+    for each in row_sums:
+        each.end()
+    for number, out in enumerate((block_out, token_grad)):
+        links.got(out.at[other_rows, :], i_out + number)
+    links.sent(first_low, s_out)
+    links.sent(seven, s_vec[1])
+    links.sent(seven, s_vec[2])
+
+
+def results_kernel(cols, hidden, *refs):
+    qkv, down, up, output, block, token, vec = refs[:7]
+    outs, small, wide, sems = refs[7:15], refs[15:22], refs[22:28], refs[28]
+    writes = [
+        pltpu.make_async_copy(src, dst, sems.at[n])
+        for n, (src, dst) in enumerate(zip((block, token, *wide), outs, strict=True))
+    ]
+    writes[0].start()
+    writes[1].start()
+    for n in range(3):
+        wide[n][...] = qkv[:, n * cols : (n + 1) * cols].astype(F32)
+        writes[2 + n].start()
+    for n, grads in enumerate((down, up, output)):
+        wide[3 + n][...] = grads[...].astype(F32)
+        writes[5 + n].start()
+    small[0][...] = vec[6, 0:hidden]
+    for n, out in enumerate(small[1:]):
+        out[...] = vec[n, :]
+    for write in writes:
+        write.wait()
 
 
 def kernel_shards(*args):
@@ -1092,7 +1073,8 @@
     halves = [(r // 2, n) for r, n in grads]
     any_space = pl.BlockSpec(memory_space=pl.ANY)
     in_vmem = pl.BlockSpec(memory_space=pltpu.VMEM)
-    scratch = [
+    scratch = [vmem(args[n].shape, args[n].dtype) for n in (1, 7, 9, 10, 11, 12, 13, 14)]
+    scratch += [
         vmem((n_rows, width), BF16),
         vmem((n_rows, width), BF16),
         vmem((width, cols), BF16),
@@ -1118,52 +1100,50 @@
         vmem((n_rows, 3 * cols), BF16),
     ]
     scratch += [vmem(s, BF16) for s in grads]
-    for _ in range(4):
+    for _ in range(3):
         scratch += [vmem(s, BF16) for s in halves]
     scratch += [
         vmem((8, width), F32),
         vmem((8, width), F32),
         vmem((8, 8, width // 8), F32),
         vmem((8, width // 8), F32),
-        vmem((8, width), F32),
-        pltpu.SemaphoreType.DMA((N_SEMS,)),
-        pltpu.SemaphoreType.DMA((N_SEMS,)),
-        pltpu.SemaphoreType.DMA((48,)),
+        pltpu.SemaphoreType.DMA((N_SENDS,)),
+        pltpu.SemaphoreType.DMA((N_RECVS,)),
+        pltpu.SemaphoreType.DMA((N_LOCAL,)),
     ]
     block_out, token_grad, down, up, output, qkv, vec = pl.pallas_call(
         functools.partial(layer_kernel, count),
         out_shape=[
-            jax.ShapeDtypeStruct((n_rows, width), BF16),
-            jax.ShapeDtypeStruct((n_rows, width), BF16),
-            *[jax.ShapeDtypeStruct(s, BF16) for s in grads],
-            jax.ShapeDtypeStruct((8, width), F32),
+            vmem((n_rows, width), BF16),
+            vmem((n_rows, width), BF16),
+            *[vmem(s, BF16) for s in grads],
+            vmem((8, width), F32),
         ],
-        in_specs=[any_space if a.ndim == 2 else in_vmem for a in args],
-        out_specs=[any_space] * 6 + [in_vmem],
+        in_specs=[any_space] * len(args),
+        out_specs=[in_vmem] * 7,
         scratch_shapes=scratch,
         compiler_params=pltpu.CompilerParams(
-            collective_id=0, has_side_effects=True, vmem_limit_bytes=63 * 2**20
+            collective_id=0, has_side_effects=True, vmem_limit_bytes=54 * 2**20
         ),
         name="layer",
     )(*args)
 
-    blocks = 4
-    by_rows = [pl.BlockSpec((r // blocks, n), lambda i: (i, 0)) for r, n in grads]
-    apart = pl.BlockSpec((width // blocks, cols), lambda i: (i, 0))
-    f32_grads = [jax.ShapeDtypeStruct(s, F32) for s in grads]
-    split = jax.ShapeDtypeStruct((width, cols), F32)
+    split = (width, cols)
+    f32_grads = [split] * 3 + list(grads[:3])
     vector = jax.ShapeDtypeStruct((width,), F32)
-    query, key, value, output, up, up_bias, down, *vectors = pl.pallas_call(
-        functools.partial(results_kernel, cols, hidden, blocks),
-        grid=(blocks,),
-        out_shape=[split] * 3
-        + [f32_grads[2], f32_grads[1], jax.ShapeDtypeStruct((hidden,), F32), f32_grads[0]]
+    rows = (n_rows, width)
+    block_out, token_grad, query, key, value, down, up, output, up_bias, *vectors = pl.pallas_call(
+        functools.partial(results_kernel, cols, hidden),
+        out_shape=[jax.ShapeDtypeStruct(rows, BF16)] * 2
+        + [jax.ShapeDtypeStruct(s, F32) for s in f32_grads]
+        + [jax.ShapeDtypeStruct((hidden,), F32)]
         + [vector] * 6,
-        in_specs=by_rows + [in_vmem],
-        out_specs=[apart] * 3 + [by_rows[2], by_rows[1], in_vmem, by_rows[0]] + [in_vmem] * 6,
-        compiler_params=pltpu.CompilerParams(vmem_limit_bytes=48 * 2**20),
+        in_specs=[in_vmem] * 7,
+        out_specs=[any_space] * 8 + [in_vmem] * 7,
+        scratch_shapes=[vmem(s, F32) for s in f32_grads] + [pltpu.SemaphoreType.DMA((8,))],
+        compiler_params=pltpu.CompilerParams(vmem_limit_bytes=16 * 2**20),
         name="results",
-    )(down, up, output, qkv, vec)
+    )(qkv, down, up, output, block_out, token_grad, vec)
     return (
         block_out,
         token_grad,

time: 127 us -> 113 us (0.89)
  local copies, waits for them, and re-layouts: 9.17 us -> 0 us
  Pallas kernels: 117 us -> 112 us
    unnamed x16 -> x0, local copies, waits for them, and re-layouts: 9.17 us -> none
    pallas_call x2, Pallas kernels: 117 us -> 112 us  [the longest x1 107 us: kernel_shards(): pl.pallas_call(functools.partial(layer_kernel, count), out_shape=[vmem((n...]
where the time goes in v3:
time: 113 us
  Pallas kernels  112 us (99%)
    pallas_call x1, Pallas kernels, kernel_shards(): pl.pallas_call(functools.partial(layer_kernel, count), out_shape=[vmem((n...  107 us
    pallas_call x1, Pallas kernels, kernel_shards(): pl.pallas_call(functools.partial(results_kernel, cols, hidden), out_shape...  5.2 us

profile of v3, /device:TPU:0, one launch (start us, length us, event | category | flops | bytes accessed | tf_op | source)
XLA Modules:
  0.0 112.6 jit_solution(6485160141766161743)
XLA Ops:
  0.7 106.6 %layer.1 = (bf16[960,1024]{1,0:T(8,128)(2,1)S(1)}, bf16[960,1024]{1,0:T(8,128)(2,1)S(1)}, bf16[512,1024]{1,0:T(8,128)(2,1)S(1)}, bf16[1024,512]{1,0:T(8,128)(2,1...) custom-call(bf16[960,1024]{1,0:T(8,128)(2,1)} %tokens_hbm.1, ...), custom_call_target="tpu_custom_call" | custom-call | tf_op jit(solution)/shard_map/layer/pallas_call | solution.py:1114
  107.2 5.2 %results.1 = (bf16[960,1024]{1,0:T(8,128)(2,1)}, bf16[960,1024]{1,0:T(8,128)(2,1)}, f32[1024,256]{1,0:T(8,128)}, f32[1024,256]{1,0:T(8,128)}, f32[1024,256]{1,0:...) custom-call(bf16[1024,768]{1,0:T(8,128)(2,1)S(1)} %get-tuple-element, ...), custom_call_target="tpu_custom_call" | custom-call | tf_op jit(solution)/shard_map/results/pallas_call | solution.py:1135

commit v4 on v3

--- a/solution.py
+++ b/solution.py
@@ -261,29 +261,38 @@
 F32 = jnp.float32
 BF16 = jnp.bfloat16
 MESH = pl.DeviceIdType.MESH
-N_SENDS = 32
-N_RECVS = 128
 N_LOCAL = 19
 
+TASKS = "DUOQSTVWFGBAXYZHKPE"
 PARTS = (
-    ("D", 0, 128, "d"), ("D", 128, 128, "a"), ("D", 256, 128, "a"), ("D", 384, 128, "a"),
-    ("U", 0, 256, "d"), ("U", 256, 256, "d"), ("U", 512, 256, "a"), ("U", 768, 256, "a"),
-    ("O", 0, 128, "a"), ("O", 128, 128, "a"), ("Q", 0, 128, "a"), ("Q", 128, 128, "d"),
-    ("Q", 256, 128, "a"), ("Q", 384, 128, "a"), ("Q", 512, 128, "d"), ("Q", 640, 128, "d"),
-    ("Q", 768, 128, "d"), ("Q", 896, 128, "a"),
+    ("D", 0, 64, "a"), ("D", 64, 64, "d"), ("D", 128, 64, "a"), ("D", 192, 64, "a"),
+    ("D", 256, 64, "d"), ("D", 320, 64, "a"), ("D", 384, 64, "a"), ("D", 448, 64, "a"),
+    ("U", 0, 128, "a"), ("U", 128, 128, "d"), ("U", 256, 128, "d"), ("U", 384, 128, "a"),
+    ("U", 512, 128, "a"), ("U", 640, 128, "a"), ("U", 768, 128, "b"), ("U", 896, 128, "a"),
+    ("O", 0, 64, "a"), ("O", 64, 64, "b"), ("O", 128, 64, "a"), ("O", 192, 64, "d"),
+    ("Q", 0, 64, "d"), ("Q", 64, 64, "a"), ("Q", 128, 64, "a"), ("Q", 192, 64, "a"),
+    ("Q", 256, 64, "a"), ("Q", 320, 64, "a"), ("Q", 384, 64, "a"), ("Q", 448, 64, "d"),
+    ("Q", 512, 64, "a"), ("Q", 576, 64, "a"), ("Q", 640, 64, "d"), ("Q", 704, 64, "d"),
+    ("Q", 768, 64, "a"), ("Q", 832, 64, "a"), ("Q", 896, 64, "a"), ("Q", 960, 64, "d"),
 )
 ORDER = (
-    "P0", "E0", "P1", "E2", "E1", "V0", "S0", "E3", "U0", "D0", "S1", "U3", "T0", "D1", "U2", "T1",
-    "V1", "U1", "W0", "4.1", "1.1", "0.1", "7.1", "4.2", "5.1", "2.1", "e4.3", "0.2", "1.2", "3.1",
-    "B0", "5.2", "A0", "e0.3", "7.2", "6.1", "A1", "1.3", "F0", "e5.3", "e4.4", "2.2", "G0",
-    "e1.4", "e0.4", "7.3", "3.2", "2.3", "6.2", "B1", "e5.4", "e7.4", "A2", "3.3", "4.5", "A3",
-    "e2.4", "Q2", "6.3", "O0", "Q3", "Q0", "0.5", "F1", "e3.4", "Q1", "4.6", "5.5", "G1", "W1",
-    "e6.4", "0.6", "14.1", "X0", "8.1", "15.1", "5.6", "16.1", "9.1", "14.2", "11.1", "17.1",
-    "15.2", "10.1", "e14.3", "e15.3", "16.2", "8.2", "12.1", "e16.3", "Y0", "11.2", "9.2", "13.1",
-    "e11.3", "e8.4", "e14.4", "e9.4", "8.3", "17.2", "10.2", "9.3", "12.2", "17.3", "13.2", "10.3",
-    "Y1", "Z0", "e15.4", "e17.4", "12.3", "Z1", "e16.4", "e10.4", "e11.4", "14.5", "13.3", "15.5",
-    "14.6", "Z2", "e12.4", "e13.4", "16.5", "15.6", "11.5", "X1", "16.6", "11.6",
+    1150, 1151, 1160, 1161, 1162, 1163, 1170, 1180, 1171, 1182, 1181, 1040, 1060, 1183, 1011, 1001,
+    1041, 1061, 1050, 1000, 1010, 1013, 101, 111, 1051, 1070, 1012, 41, 51, 61, 11, 102, 71, 91,
+    42, 1, 103, 12, 21, 43, 141, 92, 31, 13, 112, 81, 93, 52, 142, 1100, 151, 62, 113, 1110, 121,
+    53, 72, 1111, 2, 63, 131, 1080, 114, 104, 54, 44, 22, 143, 73, 32, 1090, 64, 14, 94, 74, 3, 82,
+    23, 152, 144, 122, 1101, 4, 1112, 24, 132, 33, 83, 1113, 153, 105, 1031, 45, 1032, 123, 1081,
+    34, 15, 1033, 1030, 133, 1020, 84, 95, 1091, 271, 106, 1071, 154, 241, 301, 46, 251, 124, 311,
+    16, 1120, 134, 261, 351, 96, 281, 201, 272, 291, 302, 171, 312, 321, 352, 191, 331, 202, 242,
+    341, 273, 252, 172, 211, 303, 262, 221, 313, 192, 282, 231, 353, 243, 1130, 203, 292, 253, 322,
+    263, 161, 332, 283, 342, 181, 193, 244, 254, 264, 284, 294, 324, 274, 304, 314, 293, 212, 323,
+    173, 222, 333, 232, 343, 162, 213, 182, 174, 1131, 334, 223, 275, 1140, 354, 344, 204, 214,
+    233, 305, 1141, 194, 224, 234, 315, 163, 355, 183, 205, 276, 306, 1142, 164, 184, 195, 316,
+    356, 206, 1121, 196,
 )
+
+N_ROWS = {name: sum(p[2] for p in PARTS if p[0] == name) for name in "DUOQ"}
+N_SENDS = len({(p[0], p[3], p[1] * 3 // N_ROWS[p[0]]) for p in PARTS}) + 11
+N_RECVS = 3 * len(PARTS) + 38
 
 
 def dot(a, b):
@@ -451,7 +460,8 @@
     links = Links(sends, recvs, sib)
 
     barrier = pltpu.get_barrier_semaphore()
-    for peer in [sib, opp, diag] + dp_peers:
+    peers = [sib, opp, diag, (adj[0], t_sib), (xp[0], t_sib)] + dp_peers
+    for peer in peers:
         pl.semaphore_signal(barrier, inc=1, device_id=peer, device_id_type=MESH)
 
     other_rows = span((1 - c) * half, half)
@@ -527,8 +537,8 @@
         return wo_all.at[span(t_opp * cols + number * piece + which * piece // 2, piece // 2), :]
 
     from_x, from_z = half_piece(q_xp, 0), half_piece(q_adj, 1)
-    on_z = links.copy(from_x, from_x, s_wo, i_wo + 4, adj)
-    on_x = links.copy(from_z, from_z, s_wo, i_wo + 5, xp)
+    on_z = [links.copy(from_x, from_x, s_wo, i_wo + 4, (adj[0], v)) for v in (t, t_sib)]
+    on_x = [links.copy(from_z, from_z, s_wo, i_wo + 5, (xp[0], v)) for v in (t, t_sib)]
 
     def relay(number):
         part = wo_piece(t_opp, number)
@@ -542,20 +552,20 @@
 
     def share_next():
         links.got(wo_piece(t_opp, q_xp), i_wo + 2)
-        on_z.start()
+        for each in on_z:
+            each.start()
         links.got(wo_piece(t_opp, q_adj), i_wo + 3)
-        on_x.start()
+        for each in on_x:
+            each.start()
         relay(q_xp)
         relay(q_adj)
 
     def share_last():
-        links.got(half_piece(q_cross, 0), i_wo + 4)
-        links.got(half_piece(q_cross, 1), i_wo + 5)
-        relay(q_cross)
-        links.got(wo_all.at[span(t_sib * cols, cols), :], i_wo + 1)
-        links.got(wo_all.at[span(t_diag * cols, cols), :], i_wo + 6)
-
-    pl.semaphore_wait(barrier, 10)
+        links.got(wo_piece(t_opp, q_cross), i_wo + 4)
+        links.got(wo_piece(t_diag, q_cross), i_wo + 5)
+        links.got(wo_all.at[span(t_diag * cols, 3 * piece), :], i_wo + 6)
+
+    pl.semaphore_wait(barrier, len(peers))
     by_y.start()
     whole_to_sib.start()
 
@@ -578,11 +588,15 @@
         seen = jnp.logical_and(live, col_at <= row_at)
         return jnp.logical_and(same, jnp.logical_or(seen, col_at == row_at))
 
-    i_heads = links.take(half_tiles)
+    i_heads = links.take(2 * half_tiles + 1)
+    i_near = i_heads + half_tiles + 1
     s_heads = links.group()
 
     def head_slot(j):
         return span(j * tile, tile)
+
+    cut = tile // 32 * 16 + 16
+    pieces = [[(0, tile)]] * (half_tiles - 1) + [[(0, cut), (cut, tile - cut)]]
 
     def attend(i, _):
         h, j = i % 2, i // 2
@@ -614,17 +628,34 @@
             share = numerator / jnp.sum(numerator, axis=-1, keepdims=True)
             probs[number * heads_here + head] = share
             heads_own[rows, at] = dot(share.astype(BF16), v[:, at]).astype(BF16)
-        slot = heads_full.at[head_slot(j), lanes(t * cols, cols)]
+        mine = lanes(t * cols, cols)
+        slot = heads_full.at[head_slot(j), mine]
+
+        def over_y(device):
+            @pl.when(j < half_tiles - 1)
+            def _():
+                links.copy(heads_own.at[rows, :], slot, s_heads, i_heads + j, device).start()
+
+            @pl.when(j == half_tiles - 1)
+            def _():
+                for n, (start, size) in enumerate(pieces[-1]):
+                    links.copy(
+                        heads_own.at[span(h * half + j * tile + start, size), :],
+                        heads_full.at[span(j * tile + start, size), mine],
+                        s_heads,
+                        i_heads + j + n,
+                        device,
+                    ).start()
 
         @pl.when(h == c)
         def _():
-            heads_full[head_slot(j), lanes(t * cols, cols)] = heads_own[rows, :]
-            links.copy(heads_own.at[rows, :], slot, s_heads, i_heads + j, opp).start()
+            heads_full[head_slot(j), mine] = heads_own[rows, :]
+            over_y(opp)
 
         @pl.when(h != c)
         def _():
-            links.copy(heads_own.at[rows, :], slot, s_heads, i_heads + j, sib).start()
-            links.copy(heads_own.at[rows, :], slot, s_heads, i_heads + j, diag).start()
+            links.copy(heads_own.at[rows, :], slot, s_heads, i_near + j, sib).start()
+            over_y(diag)
 
         @pl.when(i == 1)
         def _():
@@ -636,63 +667,116 @@
 
     share_next()
 
-    i_second = links.take(half_tiles)
+    i_second = links.take(half_tiles + 1)
     s_second = links.group()
     vec[...] = jnp.zeros_like(vec)
 
     def in_turn(i):
         return jnp.where(i % 2 == 0, own_start, sib_start) + (i // 2) * tile
 
-    def feed(i):
-        rows = span(in_turn(i), tile)
-        if i % 2 == 1:
-            links.got(second_low.at[rows, :], i_second + i // 2)
-        u = dot(second_low[rows, :], up_weight[...]) + row(up_bias)
-        big = 0.5 * (1.0 + lax.erf(u * (1.0 / math.sqrt(2.0))))
-        act[rows, :] = (u * big).astype(BF16)
-        slope = big + u * (jnp.exp(-0.5 * u * u) * (1.0 / math.sqrt(2.0 * math.pi)))
-        grad = (dot_nt(cotangent[rows, :], down_weight[...]) * slope).astype(BF16)
-        ugp[rows, :] = grad
-        vec[6:7, 0:hidden] += jnp.sum(grad.astype(F32), axis=0, keepdims=True)
-
-    def project(j):
+    chip = 2 * cols
+    own_k, other_k = lanes((t // 2) * chip, chip), lanes((1 - t // 2) * chip, chip)
+
+    def prepare(j):
+        here = head_slot(j)
         if j == 0:
             for load in loads[early:]:
                 load.wait()
+            links.got(wo_all.at[span(t_sib * cols, cols), :], i_wo + 1)
+        links.got(heads_full.at[here, lanes(t_sib * cols, cols)], i_near + j)
+        residual[here, :] = dot(heads_full[here, own_k], wo_all[span((t // 2) * chip, chip), :])
+
+    def down_slot(i):
+        return residual_grad.at[head_slot(i // 2), (i % 2) * hidden : (i % 2 + 1) * hidden]
+
+    def prepare_feed(i):
+        down_slot(i)[...] = dot_nt(cotangent[span(in_turn(i), tile), :], down_weight[...])
+
+    def feed(i):
+        here = pieces[i // 2] if i % 2 == 1 else [(0, tile)]
+        for n, (start, size) in enumerate(here):
+            rows = span(in_turn(i) + start, size)
+            if i % 2 == 1:
+                links.got(second_low.at[rows, :], i_second + i // 2 + n)
+            u = dot(second_low[rows, :], up_weight[...]) + row(up_bias)
+            big = 0.5 * (1.0 + lax.erf(u * (1.0 / math.sqrt(2.0))))
+            act[rows, :] = (u * big).astype(BF16)
+            slope = big + u * (jnp.exp(-0.5 * u * u) * (1.0 / math.sqrt(2.0 * math.pi)))
+            grad = (down_slot(i)[start : start + size, :] * slope).astype(BF16)
+            ugp[rows, :] = grad
+            vec[6:7, 0:hidden] += jnp.sum(grad.astype(F32), axis=0, keepdims=True)
+
+    def project(j):
+        if j == 0:
             share_last()
-        here = head_slot(j)
-        links.got(heads_full.at[here, 0 : 3 * cols], i_heads + j)
-        rows = span(own_start + j * tile, tile)
-        v = tokens[rows, :].astype(F32) + dot(heads_full[here, :], wo_all[...]) + row(output_bias)
-        residual[here, :] = v
-        xhat, _r = norm_parts(v)
-        second_low[rows, :] = (xhat * row(second_gain) + row(second_shift)).astype(BF16)
-        links.copy(
-            second_low.at[rows, :], second_low.at[rows, :], s_second, i_second + j, sib
-        ).start()
+        for n, (start, size) in enumerate(pieces[j]):
+            here = span(j * tile + start, size)
+            links.got(heads_full.at[here, other_k], i_heads + j + n)
+            rows = span(own_start + j * tile + start, size)
+            other = dot(heads_full[here, other_k], wo_all[span((1 - t // 2) * chip, chip), :])
+            v = tokens[rows, :].astype(F32) + (residual[here, :] + other) + row(output_bias)
+            residual[here, :] = v
+            xhat, _r = norm_parts(v)
+            second_low[rows, :] = (xhat * row(second_gain) + row(second_shift)).astype(BF16)
+            links.copy(
+                second_low.at[rows, :], second_low.at[rows, :], s_second, i_second + j + n, sib
+            ).start()
 
     class Tensor:
-        def __init__(self, grads, rx, rz, rm, out):
+        def __init__(self, grads, rx, rz, rm, out, long):
             self.grads, self.rx, self.rz, self.rm, self.out = grads, rx, rz, rm, out
+            self.long = long
+            self.final = links.take()
+            self.groups = {}
+
+        def group_of(self, kind, start):
+            key = kind, start * 3 // self.grads.shape[0]
+            if key not in self.groups:
+                self.groups[key] = links.group()
+            return self.groups[key]
+
+        def end(self, name):
+            mine = [p for p in PARTS if p[0] == name]
+            halves = {kind: sum(p[2] // 2 for p in mine if p[3] == kind) for kind in "abcdh"}
+            for here, copies, came in (
+                (is_mid, {"a": 4, "b": 5, "c": 4, "d": 4, "h": 4}, {"a": 1, "b": 0, "c": 1, "d": 0, "h": 1}),
+                (is_end, {"a": 3, "b": 2, "c": 3, "d": 3, "h": 3}, {"a": 1, "b": 2, "c": 1, "d": 1, "h": 1}),
+            ):
+
+                @pl.when(here)
+                def _(copies=copies, came=came):
+                    rows = sum(came[kind] * halves[kind] for kind in "abcdh")
+                    assert rows <= self.long.shape[0]
+                    if rows > 0:
+                        links.got(self.long.at[0:rows, :], self.final)
+                    for (kind, which), group in self.groups.items():
+                        rows = sum(
+                            copies[kind] * p[2] // 2
+                            for p in mine
+                            if p[3] == kind and p[1] * 3 // self.grads.shape[0] == which
+                        )
+                        assert rows <= self.long.shape[0]
+                        links.sent(self.long.at[0:rows, :], group)
 
     tensors = {
-        "D": Tensor(g_down, rx_down, rz_down, rm_down, down_out),
-        "U": Tensor(g_up, rx_up, rz_up, rm_up, up_out),
-        "O": Tensor(g_output, rx_output, rz_output, rm_output, output_out),
-        "Q": Tensor(g_qkv, rx_qkv, rz_qkv, rm_qkv, qkv_out),
+        "D": Tensor(g_down, rx_down, rz_down, rm_down, down_out, wo_all),
+        "U": Tensor(g_up, rx_up, rz_up, rm_up, up_out, up_weight),
+        "O": Tensor(g_output, rx_output, rz_output, rm_output, output_out, wo_all),
+        "Q": Tensor(g_qkv, rx_qkv, rz_qkv, rm_qkv, qkv_out, dqkv),
     }
 
     class Part:
-        def __init__(self, tensor, start, size):
+        def __init__(self, tensor, start, size, kind):
             self.size = size // 2
             self.start = start
             here = pl.ds(start // 2, self.size)
             self.grads, self.out = tensor.grads, tensor.out
-            self.rx, self.rz, self.rm = (
-                ref.at[here, :] for ref in (tensor.rx, tensor.rz, tensor.rm)
-            )
-            self.index = links.take(4)
-            self.group = links.group()
+            self.rx, self.rm = tensor.rx.at[here, :], tensor.rm.at[here, :]
+            self.rz = tensor.rz.at[pl.ds(start, self.size), :]
+            self.rz_whole = tensor.rz.at[pl.ds(start, size), :]
+            self.index = links.take(3)
+            self.final = tensor.final
+            self.group = tensor.group_of(kind, start)
 
         def half_at(self, which):
             return span(self.start + which * self.size, self.size)
@@ -700,14 +784,14 @@
         def send(self, src, dst, message, device):
             links.copy(src, dst, self.group, self.index + message, device).start()
 
+        def send_last(self, ref, device):
+            links.copy(ref, ref, self.group, self.final, device).start()
+
         def got(self, dst, message):
             links.got(dst, self.index + message)
 
         def add(self, rows, came):
             return (self.grads[rows, :].astype(F32) + came[...].astype(F32)).astype(BF16)
-
-        def sent(self, copies):
-            links.sent(self.grads.at[0 : copies * self.size, :], self.group)
 
     class PartX(Part):
         def begin(self):
@@ -739,25 +823,104 @@
                     self.got(self.rm, 2)
                     self.out[mine, :] = self.add(mine, self.rm)
                     self.send(out, out, 1, adj)
-                    self.send(out, out, 3, xp)
+                    self.send_last(out, xp)
 
             if number == 4:
 
                 @pl.when(is_end)
                 def _():
                     self.got(out, 1)
-                    self.send(out, out, 3, xp)
-
-        def end(self):
-            self.got(self.out.at[self.half_at(1 - x), :], 3)
-
+                    self.send_last(out, xp)
+
+    class PartE(Part):
+        def begin(self):
+            self.send(self.grads.at[self.half_at(1 - x), :], self.rx, 0, xp)
+
+        def step(self, number):
+            size = self.size // 2
+            mine = self.half_at(x)
+            near = span(self.start + x * self.size + side * size, size)
+            far = span(self.start + x * self.size + (1 - side) * size, size)
+            near_out, far_out = self.out.at[near, :], self.out.at[far, :]
+            rz, rm = self.rz.at[0:size, :], self.rm.at[0:size, :]
+            if number == 1:
+                self.got(self.rx, 0)
+                self.grads[mine, :] = self.add(mine, self.rx)
+
+            @pl.when(is_end if number in (1, 4, 7) else is_mid)
+            def _():
+                if number == 1:
+                    self.send(self.grads.at[far, :], rz, 1, adj)
+                if number == 2:
+                    self.got(rz, 1)
+                    self.grads[far, :] = self.add(far, rz)
+                    self.send(self.grads.at[far, :], rm, 2, mid)
+                if number == 3:
+                    self.got(rm, 2)
+                    self.grads[near, :] = self.add(near, rm)
+                    self.send(self.grads.at[near, :], rz, 1, adj)
+                if number == 4:
+                    self.got(rz, 1)
+                    self.out[near, :] = self.add(near, rz)
+                    self.send(near_out, near_out, 0, adj)
+                    self.send_last(near_out, xp)
+                if number == 5:
+                    self.got(near_out, 0)
+                    self.send(near_out, near_out, 1, mid)
+                    self.send_last(near_out, xp)
+                if number == 6:
+                    self.got(far_out, 1)
+                    self.send(far_out, far_out, 0, adj)
+                    self.send_last(far_out, xp)
+                if number == 7:
+                    self.got(far_out, 0)
+                    self.send_last(far_out, xp)
+
+    class PartH(Part):
+        def begin(self):
             @pl.when(is_end)
             def _():
-                self.sent(3)
-
-            @pl.when(is_mid)
+                whole = self.grads.at[pl.ds(self.start, 2 * self.size), :]
+                self.send(whole, self.rz_whole, 0, adj)
+
+        def step(self, number):
+            size = self.size // 2
+            near, far = self.half_at(side), self.half_at(1 - side)
+            near_at = self.start + side * self.size
+            far_at = self.start + (1 - side) * self.size
+            near_mine = span(near_at + x * size, size)
+            near_other = span(near_at + (1 - x) * size, size)
+            far_mine = span(far_at + x * size, size)
+            near_out, far_out = self.out.at[near_mine, :], self.out.at[far_mine, :]
+            rx = self.rx.at[0:size, :]
+
+            @pl.when(is_end if number > 4 else is_mid)
             def _():
-                self.sent(4)
+                if number == 1:
+                    whole = pl.ds(self.start, 2 * self.size)
+                    self.got(self.rz_whole, 0)
+                    self.grads[whole, :] = self.add(whole, self.rz_whole)
+                    self.send(self.grads.at[far, :], self.rm, 1, mid)
+                if number == 2:
+                    self.got(self.rm, 1)
+                    self.grads[near, :] = self.add(near, self.rm)
+                    self.send(self.grads.at[near_other, :], rx, 2, xp)
+                if number == 3:
+                    self.got(rx, 2)
+                    self.out[near_mine, :] = self.add(near_mine, rx)
+                    self.send(near_out, near_out, 0, adj)
+                    self.send(near_out, near_out, 0, mid)
+                    self.send_last(near_out, xp)
+                if number == 4:
+                    self.got(far_out, 0)
+                    self.send(far_out, far_out, 1, adj)
+                    self.send_last(far_out, xp)
+                if number == 5:
+                    self.got(near_out, 0)
+                    self.send_last(near_out, xp)
+                if number == 6:
+                    self.got(far_out, 1)
+                    self.send_last(far_out, xp)
 
     class PartZ(Part):
         def begin(self):
@@ -769,6 +932,7 @@
 
         def step(self, number):
             near, far = self.half_at(side), self.half_at(1 - side)
+            near_out, far_out = self.out.at[near, :], self.out.at[far, :]
 
             @pl.when(is_end if number in (3, 4) else is_mid)
             def _():
@@ -787,28 +951,47 @@
                 if number == 4:
                     self.got(self.rx, 1)
                     self.out[near, :] = self.add(near, self.rx)
-                    self.send(self.out.at[near, :], self.out.at[near, :], 2, adj)
+                    self.send(near_out, near_out, 0, adj)
                 if number == 5:
-                    self.got(self.out.at[near, :], 2)
-                    self.send(self.out.at[near, :], self.out.at[near, :], 3, mid)
+                    self.got(near_out, 0)
+                    self.send(near_out, near_out, 2, mid)
                 if number == 6:
-                    self.got(self.out.at[far, :], 3)
-                    self.send(self.out.at[far, :], self.out.at[far, :], 2, adj)
-
-        def end(self):
-            near, far = self.half_at(side), self.half_at(1 - side)
-
+                    self.got(far_out, 2)
+                    self.send_last(far_out, adj)
+
+    class PartM(Part):
+        def begin(self):
             @pl.when(is_end)
             def _():
-                self.got(self.out.at[far, :], 2)
-                self.sent(3)
+                whole = self.grads.at[pl.ds(self.start, 2 * self.size), :]
+                self.send(whole, self.rz_whole, 0, adj)
+
+        def step(self, number):
+            near, far = self.half_at(side), self.half_at(1 - side)
+            near_out, far_out = self.out.at[near, :], self.out.at[far, :]
 
             @pl.when(is_mid)
             def _():
-                self.sent(4)
+                if number == 1:
+                    whole = pl.ds(self.start, 2 * self.size)
+                    self.got(self.rz_whole, 0)
+                    self.grads[whole, :] = self.add(whole, self.rz_whole)
+                    self.send(self.grads.at[far, :], self.rm, 1, mid)
+                if number == 2:
+                    self.got(self.rm, 1)
+                    self.grads[near, :] = self.add(near, self.rm)
+                    self.send(self.grads.at[near, :], self.rx, 2, xp)
+                if number == 3:
+                    self.got(self.rx, 2)
+                    self.out[near, :] = self.add(near, self.rx)
+                    self.send_last(near_out, adj)
+                    self.send(near_out, near_out, 0, mid)
+                if number == 4:
+                    self.got(far_out, 0)
+                    self.send_last(far_out, adj)
 
     parts = [
-        {"a": PartX, "d": PartZ}[kind](tensors[name], start, size)
+        {"a": PartX, "b": PartM, "c": PartE, "d": PartZ, "h": PartH}[kind](tensors[name], start, size, kind)
         for name, start, size, kind in PARTS
     ]
 
@@ -839,8 +1022,9 @@
         begin_parts("Q", i * block, block)
 
     class RowSum:
-        def __init__(self, number, part):
-            self.snd, self.r1, self.cs, self.r2 = (mail.at[4 * number + n] for n in range(4))
+        def __init__(self, number, part, snd):
+            self.snd = snd
+            self.r1, self.cs, self.r2 = (mail.at[3 * number + n] for n in range(3))
             self.part = part
             self.index = links.take(2 * half_tiles)
             self.group = links.group()
@@ -873,13 +1057,14 @@
         def end(self):
             links.sent(first_low, self.group)
 
-    second_sum = RowSum(0, lambda rows: dot_nt(ugp[rows, :], up_weight[...]))
-    out_sum = RowSum(1, lambda rows: dot(act[rows, :], down_weight[...]))
+    second_sum = RowSum(0, lambda rows: dot_nt(ugp[rows, :], up_weight[...]), mail.at[9])
+    out_sum = RowSum(1, lambda rows: dot(act[rows, :], down_weight[...]), mail.at[10])
     first_sum = RowSum(
         2,
         lambda rows: dot_nt(dqkv[rows, 0:cols], query_weight[...])
         + dot_nt(dqkv[rows, cols : 2 * cols], key_weight[...])
         + dot_nt(dqkv[rows, 2 * cols : 3 * cols], value_weight[...]),
+        heads_full,
     )
     row_sums = (second_sum, out_sum, first_sum)
 
@@ -1011,20 +1196,21 @@
         "X": finish_out,
         "Y": first_back,
         "Z": vectors,
+        "H": prepare,
+        "K": prepare_feed,
         "P": project,
         "E": feed,
     }
-    for name in ORDER:
-        if "." in name:
-            number, step = name.removeprefix("e").split(".")
-            parts[int(number)].step(int(step))
+    for code in ORDER:
+        if code < 1000:
+            parts[code // 10].step(code % 10)
         else:
-            tasks[name[0]](int(name[1:]))
+            tasks[TASKS[code // 10 - 100]](code % 10)
 
     vectors(3)
 
-    for each in parts:
-        each.end()
+    for name, tensor in tensors.items():
+        tensor.end(name)
     links.sent(wo_all.at[0 : 3 * cols, :], s_wo)
     links.sent(heads_full.at[:, 0 : 3 * cols], s_heads)
     links.sent(second_low.at[0:half, :], s_second)
@@ -1040,22 +1226,24 @@
 
 def results_kernel(cols, hidden, *refs):
     qkv, down, up, output, block, token, vec = refs[:7]
-    outs, small, wide, sems = refs[7:15], refs[15:22], refs[22:28], refs[28]
+    outs, wide, small, sems = refs[7:22], refs[22:28], refs[28:35], refs[35]
     writes = [
         pltpu.make_async_copy(src, dst, sems.at[n])
-        for n, (src, dst) in enumerate(zip((block, token, *wide), outs, strict=True))
+        for n, (src, dst) in enumerate(zip((block, token, *wide, *small), outs, strict=True))
     ]
     writes[0].start()
     writes[1].start()
+    small[0][...] = vec[6, 0:hidden]
+    for n, ref in enumerate(small[1:]):
+        ref[...] = vec[n, :]
+    for write in writes[8:]:
+        write.start()
     for n in range(3):
         wide[n][...] = qkv[:, n * cols : (n + 1) * cols].astype(F32)
         writes[2 + n].start()
     for n, grads in enumerate((down, up, output)):
         wide[3 + n][...] = grads[...].astype(F32)
         writes[5 + n].start()
-    small[0][...] = vec[6, 0:hidden]
-    for n, out in enumerate(small[1:]):
-        out[...] = vec[n, :]
     for write in writes:
         write.wait()
 
@@ -1094,14 +1282,14 @@
         vmem((n_rows, width), BF16),
         vmem((n_rows, hidden), BF16),
         vmem((n_rows, hidden), BF16),
-        vmem((12, half, width), BF16),
+        vmem((11, half, width), BF16),
         vmem((half, width), F32),
         vmem((n_rows, width), BF16),
         vmem((n_rows, 3 * cols), BF16),
     ]
     scratch += [vmem(s, BF16) for s in grads]
-    for _ in range(3):
-        scratch += [vmem(s, BF16) for s in halves]
+    for shapes in (halves, grads, halves):
+        scratch += [vmem(s, BF16) for s in shapes]
     scratch += [
         vmem((8, width), F32),
         vmem((8, width), F32),
@@ -1123,7 +1311,7 @@
         out_specs=[in_vmem] * 7,
         scratch_shapes=scratch,
         compiler_params=pltpu.CompilerParams(
-            collective_id=0, has_side_effects=True, vmem_limit_bytes=54 * 2**20
+            collective_id=0, has_side_effects=True, vmem_limit_bytes=56 * 2**20
         ),
         name="layer",
     )(*args)
@@ -1139,8 +1327,9 @@
         + [jax.ShapeDtypeStruct((hidden,), F32)]
         + [vector] * 6,
         in_specs=[in_vmem] * 7,
-        out_specs=[any_space] * 8 + [in_vmem] * 7,
-        scratch_shapes=[vmem(s, F32) for s in f32_grads] + [pltpu.SemaphoreType.DMA((8,))],
+        out_specs=[any_space] * 15,
+        scratch_shapes=[vmem(s, F32) for s in (*f32_grads, (hidden,), *[(width,)] * 6)]
+        + [pltpu.SemaphoreType.DMA((15,))],
         compiler_params=pltpu.CompilerParams(vmem_limit_bytes=16 * 2**20),
         name="results",
     )(qkv, down, up, output, block_out, token_grad, vec)

time: 113 us -> 109 us (0.965)
  Pallas kernels: 112 us -> 108 us
    pallas_call x1, Pallas kernels: 107 us -> 104 us  [kernel_shards(): pl.pallas_call(functools.partial(layer_kernel, count), out_shape=[vmem((n...]
where the time goes in v4:
time: 109 us
  Pallas kernels  108 us (99%)
    pallas_call x1, Pallas kernels, kernel_shards(): pl.pallas_call(functools.partial(layer_kernel, count), out_shape=[vmem((n...  104 us
    pallas_call x1, Pallas kernels, kernel_shards(): pl.pallas_call(functools.partial(results_kernel, cols, hidden), out_shape...  4.68 us

profile of v4, /device:TPU:0, one launch (start us, length us, event | category | flops | bytes accessed | tf_op | source)
XLA Modules:
  0.0 109.2 jit_solution(6067567312197283658)
XLA Ops:
  0.7 103.7 %layer.1 = (bf16[960,1024]{1,0:T(8,128)(2,1)S(1)}, bf16[960,1024]{1,0:T(8,128)(2,1)S(1)}, bf16[512,1024]{1,0:T(8,128)(2,1)S(1)}, bf16[1024,512]{1,0:T(8,128)(2,1...) custom-call(bf16[960,1024]{1,0:T(8,128)(2,1)} %tokens_hbm.1, ...), custom_call_target="tpu_custom_call" | custom-call | tf_op jit(solution)/shard_map/layer/pallas_call | solution.py:1302
  104.3 4.7 %results.1 = (bf16[960,1024]{1,0:T(8,128)(2,1)}, bf16[960,1024]{1,0:T(8,128)(2,1)}, f32[1024,256]{1,0:T(8,128)}, f32[1024,256]{1,0:T(8,128)}, f32[1024,256]{1,0:...) custom-call(bf16[1024,768]{1,0:T(8,128)(2,1)S(1)} %get-tuple-element, ...), custom_call_target="tpu_custom_call" | custom-call | tf_op jit(solution)/shard_map/results/pallas_call | solution.py:1323

commit v5 on v4

--- a/solution.py
+++ b/solution.py
@@ -276,18 +276,18 @@
     ("Q", 768, 64, "a"), ("Q", 832, 64, "a"), ("Q", 896, 64, "a"), ("Q", 960, 64, "d"),
 )
 ORDER = (
-    1150, 1151, 1160, 1161, 1162, 1163, 1170, 1180, 1171, 1182, 1181, 1040, 1060, 1183, 1011, 1001,
-    1041, 1061, 1050, 1000, 1010, 1013, 101, 111, 1051, 1070, 1012, 41, 51, 61, 11, 102, 71, 91,
-    42, 1, 103, 12, 21, 43, 141, 92, 31, 13, 112, 81, 93, 52, 142, 1100, 151, 62, 113, 1110, 121,
-    53, 72, 1111, 2, 63, 131, 1080, 114, 104, 54, 44, 22, 143, 73, 32, 1090, 64, 14, 94, 74, 3, 82,
-    23, 152, 144, 122, 1101, 4, 1112, 24, 132, 33, 83, 1113, 153, 105, 1031, 45, 1032, 123, 1081,
-    34, 15, 1033, 1030, 133, 1020, 84, 95, 1091, 271, 106, 1071, 154, 241, 301, 46, 251, 124, 311,
-    16, 1120, 134, 261, 351, 96, 281, 201, 272, 291, 302, 171, 312, 321, 352, 191, 331, 202, 242,
-    341, 273, 252, 172, 211, 303, 262, 221, 313, 192, 282, 231, 353, 243, 1130, 203, 292, 253, 322,
-    263, 161, 332, 283, 342, 181, 193, 244, 254, 264, 284, 294, 324, 274, 304, 314, 293, 212, 323,
-    173, 222, 333, 232, 343, 162, 213, 182, 174, 1131, 334, 223, 275, 1140, 354, 344, 204, 214,
-    233, 305, 1141, 194, 224, 234, 315, 163, 355, 183, 205, 276, 306, 1142, 164, 184, 195, 316,
-    356, 206, 1121, 196,
+    1150, 1151, 1160, 1161, 1162, 1163, 1170, 1180, 1171, 1181, 1040, 1182, 1183, 1011, 1001, 1050,
+    1041, 1061, 101, 1000, 1060, 41, 1010, 1051, 11, 102, 1013, 91, 42, 12, 141, 111, 92, 51, 61,
+    112, 1012, 1, 103, 52, 142, 71, 62, 113, 21, 81, 93, 31, 2, 53, 72, 63, 22, 143, 1100, 43, 131,
+    82, 73, 13, 151, 3, 1110, 54, 1070, 44, 32, 132, 23, 104, 144, 114, 94, 1111, 152, 74, 83,
+    1101, 121, 33, 45, 64, 1112, 4, 133, 105, 1080, 24, 14, 95, 153, 1113, 1031, 122, 1033, 106,
+    15, 46, 1090, 271, 351, 96, 1032, 301, 1030, 16, 1081, 201, 272, 1020, 123, 311, 352, 171, 202,
+    241, 321, 191, 251, 302, 312, 1091, 242, 281, 322, 341, 172, 353, 192, 252, 282, 243, 342, 323,
+    261, 211, 221, 291, 262, 273, 253, 84, 1130, 212, 283, 343, 222, 303, 203, 231, 263, 292, 1120,
+    213, 331, 232, 274, 313, 193, 324, 223, 173, 1071, 293, 204, 332, 244, 233, 161, 154, 205, 162,
+    194, 284, 314, 174, 1131, 1140, 333, 275, 195, 224, 181, 34, 163, 182, 315, 1141, 294, 196,
+    214, 234, 124, 355, 183, 344, 354, 316, 304, 334, 264, 206, 305, 164, 1142, 1121, 356, 184,
+    306, 134, 276, 254,
 )
 
 N_ROWS = {name: sum(p[2] for p in PARTS if p[0] == name) for name in "DUOQ"}

time: 109 us -> 109 us (level)
  no operation moved by 1% of the time
where the time goes in v5:
time: 109 us; the launch traced here: 108 us
  Pallas kernels  108 us (99%)
    pallas_call x1, Pallas kernels, kernel_shards(): pl.pallas_call(functools.partial(layer_kernel, count), out_shape=[vmem((n...  103 us
    pallas_call x1, Pallas kernels, kernel_shards(): pl.pallas_call(functools.partial(results_kernel, cols, hidden), out_shape...  4.68 us

profile of v5, /device:TPU:0, one launch (start us, length us, event | category | flops | bytes accessed | tf_op | source)
XLA Modules:
  0.0 108.4 jit_solution(6848904011037625950)
XLA Ops:
  0.7 102.9 %layer.1 = (bf16[960,1024]{1,0:T(8,128)(2,1)S(1)}, bf16[960,1024]{1,0:T(8,128)(2,1)S(1)}, bf16[512,1024]{1,0:T(8,128)(2,1)S(1)}, bf16[1024,512]{1,0:T(8,128)(2,1...) custom-call(bf16[960,1024]{1,0:T(8,128)(2,1)} %tokens_hbm.1, ...), custom_call_target="tpu_custom_call" | custom-call | tf_op jit(solution)/shard_map/layer/pallas_call | solution.py:1302
  103.6 4.7 %results.1 = (bf16[960,1024]{1,0:T(8,128)(2,1)}, bf16[960,1024]{1,0:T(8,128)(2,1)}, f32[1024,256]{1,0:T(8,128)}, f32[1024,256]{1,0:T(8,128)}, f32[1024,256]{1,0:...) custom-call(bf16[1024,768]{1,0:T(8,128)(2,1)S(1)} %get-tuple-element, ...), custom_call_target="tpu_custom_call" | custom-call | tf_op jit(solution)/shard_map/results/pallas_call | solution.py:1323

commit v6 on v5

--- a/solution.py
+++ b/solution.py
@@ -276,18 +276,18 @@
     ("Q", 768, 64, "a"), ("Q", 832, 64, "a"), ("Q", 896, 64, "a"), ("Q", 960, 64, "d"),
 )
 ORDER = (
-    1150, 1151, 1160, 1161, 1162, 1163, 1170, 1180, 1171, 1181, 1040, 1182, 1183, 1011, 1001, 1050,
-    1041, 1061, 101, 1000, 1060, 41, 1010, 1051, 11, 102, 1013, 91, 42, 12, 141, 111, 92, 51, 61,
-    112, 1012, 1, 103, 52, 142, 71, 62, 113, 21, 81, 93, 31, 2, 53, 72, 63, 22, 143, 1100, 43, 131,
-    82, 73, 13, 151, 3, 1110, 54, 1070, 44, 32, 132, 23, 104, 144, 114, 94, 1111, 152, 74, 83,
-    1101, 121, 33, 45, 64, 1112, 4, 133, 105, 1080, 24, 14, 95, 153, 1113, 1031, 122, 1033, 106,
-    15, 46, 1090, 271, 351, 96, 1032, 301, 1030, 16, 1081, 201, 272, 1020, 123, 311, 352, 171, 202,
-    241, 321, 191, 251, 302, 312, 1091, 242, 281, 322, 341, 172, 353, 192, 252, 282, 243, 342, 323,
-    261, 211, 221, 291, 262, 273, 253, 84, 1130, 212, 283, 343, 222, 303, 203, 231, 263, 292, 1120,
-    213, 331, 232, 274, 313, 193, 324, 223, 173, 1071, 293, 204, 332, 244, 233, 161, 154, 205, 162,
-    194, 284, 314, 174, 1131, 1140, 333, 275, 195, 224, 181, 34, 163, 182, 315, 1141, 294, 196,
-    214, 234, 124, 355, 183, 344, 354, 316, 304, 334, 264, 206, 305, 164, 1142, 1121, 356, 184,
-    306, 134, 276, 254,
+    1150, 1151, 1160, 1161, 1162, 1163, 1170, 1171, 1182, 1181, 1040, 1180, 1183, 1011, 1001, 1050,
+    1061, 101, 1041, 1000, 41, 1010, 11, 111, 1051, 102, 91, 1060, 61, 51, 42, 1013, 112, 1012, 12,
+    71, 21, 62, 92, 31, 52, 43, 113, 1100, 141, 63, 151, 53, 72, 1, 103, 22, 1110, 32, 142, 121,
+    93, 73, 152, 23, 81, 2, 1070, 64, 33, 122, 114, 143, 1111, 104, 153, 3, 82, 1080, 44, 131, 105,
+    13, 54, 94, 1101, 123, 45, 74, 1112, 132, 34, 14, 83, 144, 24, 1113, 95, 1031, 106, 1030, 15,
+    46, 1090, 1032, 201, 1081, 133, 271, 1033, 251, 311, 16, 96, 351, 301, 272, 252, 1020, 312,
+    202, 211, 171, 1091, 124, 352, 281, 4, 191, 212, 253, 241, 302, 282, 261, 172, 321, 242, 313,
+    192, 262, 213, 283, 322, 331, 332, 221, 243, 181, 263, 222, 291, 341, 353, 203, 182, 323, 1071,
+    292, 303, 214, 173, 231, 193, 342, 354, 223, 333, 183, 204, 273, 244, 1130, 314, 161, 293, 355,
+    264, 205, 232, 174, 324, 1131, 194, 1140, 343, 284, 162, 206, 305, 356, 1120, 275, 304, 274,
+    154, 1141, 233, 195, 334, 254, 134, 184, 315, 224, 294, 163, 276, 306, 84, 1142, 1121, 316,
+    344, 164, 196, 234,
 )
 
 N_ROWS = {name: sum(p[2] for p in PARTS if p[0] == name) for name in "DUOQ"}

time: 109 us -> 108 us (level)
  no operation moved by 1% of the time
where the time goes in v6:
time: 108 us
  Pallas kernels  107 us (99%)
    pallas_call x1, Pallas kernels, kernel_shards(): pl.pallas_call(functools.partial(layer_kernel, count), out_shape=[vmem((n...  102 us
    pallas_call x1, Pallas kernels, kernel_shards(): pl.pallas_call(functools.partial(results_kernel, cols, hidden), out_shape...  4.68 us

profile of v6, /device:TPU:0, one launch (start us, length us, event | category | flops | bytes accessed | tf_op | source)
XLA Modules:
  0.0 107.8 jit_solution(16806519347016496748)
XLA Ops:
  0.7 102.3 %layer.1 = (bf16[960,1024]{1,0:T(8,128)(2,1)S(1)}, bf16[960,1024]{1,0:T(8,128)(2,1)S(1)}, bf16[512,1024]{1,0:T(8,128)(2,1)S(1)}, bf16[1024,512]{1,0:T(8,128)(2,1...) custom-call(bf16[960,1024]{1,0:T(8,128)(2,1)} %tokens_hbm.1, ...), custom_call_target="tpu_custom_call" | custom-call | tf_op jit(solution)/shard_map/layer/pallas_call | solution.py:1302
  102.9 4.7 %results.1 = (bf16[960,1024]{1,0:T(8,128)(2,1)}, bf16[960,1024]{1,0:T(8,128)(2,1)}, f32[1024,256]{1,0:T(8,128)}, f32[1024,256]{1,0:T(8,128)}, f32[1024,256]{1,0:...) custom-call(bf16[1024,768]{1,0:T(8,128)(2,1)S(1)} %get-tuple-element, ...), custom_call_target="tpu_custom_call" | custom-call | tf_op jit(solution)/shard_map/results/pallas_call | solution.py:1323
